TPU v7x, 32 devices: a whole 2x2x4 slice. The times are simulated.
32 devices in a mesh: seq: 16 (over z, x, core), batch: 2 (over y).
Axes of the slice: x: 2, y: 2, z: 4, core: 2. Of those that a mesh axis runs over, the one named last changes fastest.
Arguments:
- tokens: bfloat16 [2, 2, 2048, 512], P(None, 'batch', 'seq'), may hold values from -6 to 6
- lengths: int32 [2, 2, 64], P(None, 'batch'), may hold values from 0 to 1984, as said below
- groups: int32 [2, 2], P(None, 'batch'), may hold values from 0 to 7
- cotangent: bfloat16 [2, 2, 2048, 512], P(None, 'batch', 'seq'), may hold values from -6 to 6
- attn_weights: float32 [4, 512, 512], P(None, 'seq', 'batch')
- ffn_weights: float32 [2, 512, 2048], P(None, 'seq', 'batch')
- small_params: float32 [10240], P(('seq', 'batch'))
- attn_rows: float32 [4, 512], P(None, 'seq'), as said below
- attn_cols: float32 [4, 512], P(None, 'batch'), as said below
- ffn_rows: float32 [2, 512], P(None, 'seq'), as said below
- ffn_cols: float32 [2, 2048], P(None, 'batch'), as said below
- small_sq: float32 [10240], P(('seq', 'batch')), as said below
Outputs:
- output: bfloat16 [2, 2, 2048, 512], P(None, 'batch', 'seq')
- input_grad: bfloat16 [2, 2, 2048, 512], P(None, 'batch', 'seq')
- attn_grad: float32 [4, 512, 512], P(None, 'seq', 'batch')
- ffn_grad: float32 [2, 512, 2048], P(None, 'seq', 'batch')
- small_grad: float32 [10240], P(('seq', 'batch'))
- attn_new: float32 [4, 512, 512], P(None, 'seq', 'batch')
- ffn_new: float32 [2, 512, 2048], P(None, 'seq', 'batch')
- small_new: float32 [10240], P(('seq', 'batch'))
- attn_copy: bfloat16 [4, 512, 512], P(None, 'seq', 'batch')
- ffn_copy: bfloat16 [2, 512, 2048], P(None, 'seq', 'batch')
- small_copy: bfloat16 [10240], P(('seq', 'batch'))
- attn_rows_new: float32 [4, 512], P(None, 'seq')
- attn_cols_new: float32 [4, 512], P(None, 'batch')
- ffn_rows_new: float32 [2, 512], P(None, 'seq')
- ffn_cols_new: float32 [2, 2048], P(None, 'batch')
- small_sq_new: float32 [10240], P(('seq', 'batch'))
Inputs may be any that keep to these rules, and one draw needn't show every extreme that they name: In each row, 64 slots hold the lengths of the packed pairs in order; they sum to at most 2048; positions past the sum are filler; slots past the last pair hold 0. `attn_rows`: Positive. `attn_cols`: Positive. `ffn_rows`: Positive. `ffn_cols`: Positive. `small_sq`: Positive.
All inputs are finite; a program needn't handle non-finite values.
Results may differ from a plain program's by a relative error of at most 0.02.
Values may be sent and summed in bfloat16 or wider, within the bound.
A program may use at most 128 MiB of HBM per device.

v0:
```python
import jax
import jax.numpy as jnp
from jax import lax
from jax.sharding import PartitionSpec as P

D = 512
H = 8
HD = 64
FF = 2048
GROUPS = 8
SEGS = 64
STEP = 10
NVEC = 10240


NEG = -1e30
EPS = 1e-05
EPS_ONE = 1e-30
LEARN = 1.0
HIGHEST = lax.Precision.HIGHEST


def shortened(value):
    return jax.tree.map(lambda a: a.astype(jnp.bfloat16) if a.dtype == jnp.float32 else a, value)


def from_behind(block, axis, distance):
    devices = range(lax.axis_size(axis))
    route = [((i - distance) % len(devices), i) for i in devices]
    return lax.ppermute(block, axis, route)


def unpack_small(vector):
    widths = (D, D, D, FF, D, D, D, D, D)
    pieces = []
    offset = 0
    for amount in widths:
        pieces.append(vector[offset : offset + amount])
        offset = offset + amount
    pieces.append(vector[offset:].reshape(GROUPS, D))
    return pieces


def norm_forward(values, norm_gain, norm_shift):
    center = values - jnp.mean(values, axis=-1, keepdims=True)
    inverse = lax.rsqrt(jnp.mean(center * center, axis=-1, keepdims=True) + EPS)
    normed = center * inverse
    return (normed * norm_gain + norm_shift, normed, inverse)


def norm_backward(grad_out, normed, inverse, norm_gain):
    grad_norm = grad_out * norm_gain
    grad_in = inverse * (
        grad_norm
        - jnp.mean(grad_norm, axis=-1, keepdims=True)
        - normed * jnp.mean(grad_norm * normed, axis=-1, keepdims=True)
    )
    return (grad_in, jnp.sum(grad_out * normed, axis=0), jnp.sum(grad_out, axis=0))


def segment_rows(lengths_micro, row_length):
    row_ends = jnp.cumsum(lengths_micro, axis=-1)
    places = jnp.arange(row_length, dtype=jnp.int32)
    return jnp.sum((row_ends[:, None, :] <= places[None, :, None]).astype(jnp.int32), axis=-1)


def make_scorer(seg_rows):

    def scorer(queries, key_rows, query_start, key_start):
        rows_count, query_count = (queries.shape[0], queries.shape[1])
        key_count = key_rows.shape[1]
        query_four = queries.reshape(rows_count, query_count, H, HD)
        key_four = key_rows.reshape(rows_count, key_count, H, HD)
        scores = jnp.einsum(
            "rqhd,rkhd->rhqk", query_four, key_four, preferred_element_type=jnp.float32
        ) * HD ** (-0.5)
        seg_query = lax.dynamic_slice_in_dim(seg_rows, query_start, query_count, 1)
        seg_key = lax.dynamic_slice_in_dim(seg_rows, key_start, key_count, 1)
        pos_query = query_start + jnp.arange(query_count, dtype=jnp.int32)
        pos_key = key_start + jnp.arange(key_count, dtype=jnp.int32)
        same_pair = (seg_query[:, :, None] == seg_key[:, None, :]) & (seg_key[:, None, :] < SEGS)
        allowed = same_pair | (pos_query[:, None] == pos_key[None, :])[None]
        return (scores, allowed[:, None])

    return scorer


def fold_keys(step_fn, carry_state, pieces):
    count = pieces[0].shape[1]
    span_keys = 256

    def advance(number, running):
        offset = number * span_keys
        sliced = tuple(
            (lax.dynamic_slice_in_dim(member, offset, span_keys, 1) for member in pieces)
        )
        return step_fn(running, sliced, offset)

    return lax.fori_loop(0, count // span_keys, advance, carry_state)


def grad_block(scorer, query_side, key_side, query_start, key_start):
    queries, query_back, logsum, delta = query_side
    key_rows, value_rows = key_side
    rows_count, query_count = (queries.shape[0], queries.shape[1])
    key_count = key_rows.shape[1]
    scores, allowed = scorer(queries, key_rows, query_start, key_start)
    prob_block = jnp.where(allowed, jnp.exp(scores - logsum[..., None]), 0.0)
    back_four = query_back.reshape(rows_count, query_count, H, HD)
    value_four = value_rows.reshape(rows_count, key_count, H, HD)
    prob_grad = jnp.einsum(
        "rqhd,rkhd->rhqk", back_four, value_four, preferred_element_type=jnp.float32
    )
    score_grad = (prob_block * (prob_grad - delta[..., None])).astype(jnp.bfloat16)
    results = []
    key_four = key_rows.reshape(rows_count, key_count, H, HD)
    query_part = jnp.einsum(
        "rhqk,rkhd->rqhd", score_grad, key_four, preferred_element_type=jnp.float32
    ) * HD ** (-0.5)
    results.append(query_part.reshape(rows_count, query_count, D))
    query_four = queries.reshape(rows_count, query_count, H, HD)
    key_part = jnp.einsum(
        "rhqk,rqhd->rkhd", score_grad, query_four, preferred_element_type=jnp.float32
    ) * HD ** (-0.5)
    value_part = jnp.einsum(
        "rhqk,rqhd->rkhd",
        prob_block.astype(jnp.bfloat16),
        back_four,
        preferred_element_type=jnp.float32,
    )
    results.append(key_part.reshape(rows_count, key_count, D))
    results.append(value_part.reshape(rows_count, key_count, D))
    return results


def pass_grads(key_grad, value_grad):
    return (
        from_behind(shortened(key_grad), "seq", 1).astype(key_grad.dtype),
        from_behind(shortened(value_grad), "seq", 1).astype(value_grad.dtype),
    )


def gather_weights(attn_weights, ffn_weights, small_params):
    wide = (
        lax.all_gather(attn_weights.astype(jnp.bfloat16), "batch", axis=2, tiled=True),
        lax.all_gather(ffn_weights.astype(jnp.bfloat16), "batch", axis=2, tiled=True),
        lax.all_gather(small_params.astype(jnp.bfloat16), "batch", axis=0, tiled=True),
    )
    return (
        lax.all_gather(wide[0], "seq", axis=1, tiled=True),
        lax.all_gather(wide[1], "seq", axis=1, tiled=True),
        lax.all_gather(wide[2], "seq", axis=0, tiled=True),
    )


def scatter_grads(attn_part, ffn_part, small_part):
    rows_part = (
        lax.psum_scatter(
            attn_part.astype(jnp.bfloat16), "seq", scatter_dimension=1, tiled=True
        ).astype(jnp.float32),
        lax.psum_scatter(
            ffn_part.astype(jnp.bfloat16), "seq", scatter_dimension=1, tiled=True
        ).astype(jnp.float32),
        lax.psum_scatter(
            small_part.astype(jnp.bfloat16), "seq", scatter_dimension=0, tiled=True
        ).astype(jnp.float32),
    )
    return (
        lax.psum_scatter(
            rows_part[0].astype(jnp.bfloat16), "batch", scatter_dimension=2, tiled=True
        ).astype(jnp.float32),
        lax.psum_scatter(
            rows_part[1].astype(jnp.bfloat16), "batch", scatter_dimension=2, tiled=True
        ).astype(jnp.float32),
        lax.psum_scatter(
            rows_part[2].astype(jnp.bfloat16), "batch", scatter_dimension=0, tiled=True
        ).astype(jnp.float32),
    )


def micro_pass(
    tokens_micro, lengths_micro, groups_micro, cotangent_micro, full_weights, cycle_size, own_index
):
    attn_full, ffn_full, small_full = full_weights
    rows_local, seq_local = (tokens_micro.shape[0], tokens_micro.shape[1])
    flat_count = rows_local * seq_local
    row_length = seq_local * cycle_size
    own_start = own_index * seq_local
    (
        bias_q,
        bias_v,
        bias_o,
        bias_in,
        bias_back,
        gain_one,
        shift_one,
        gain_two,
        shift_two,
        lang_table,
    ) = unpack_small(small_full.astype(jnp.float32))
    seg_rows = segment_rows(lengths_micro, row_length)
    seg_own = lax.dynamic_slice_in_dim(seg_rows, own_start, seq_local, 1)
    live_mask = (seg_own < SEGS).astype(jnp.float32).reshape(flat_count, 1)
    one_hot = (groups_micro[:, None] == jnp.arange(GROUPS, dtype=jnp.int32)[None, :]).astype(
        jnp.float32
    )
    lang_rows = jnp.dot(one_hot, lang_table, precision=HIGHEST)
    inputs = (tokens_micro.astype(jnp.float32) + lang_rows[:, None, :]).reshape(flat_count, D)
    attn_in = inputs.astype(jnp.bfloat16)
    projected = jnp.einsum(
        "td,jde->jte", attn_in, attn_full[:3], preferred_element_type=jnp.float32
    )
    queries = (projected[0] + bias_q).astype(jnp.bfloat16).reshape(rows_local, seq_local, D)
    key_rows = projected[1].astype(jnp.bfloat16).reshape(rows_local, seq_local, D)
    value_rows = (projected[2] + bias_v).astype(jnp.bfloat16).reshape(rows_local, seq_local, D)
    scorer = make_scorer(seg_rows)

    def stats_step(carry_state, sliced, offset):
        row_peak, row_total = carry_state
        scores, allowed = scorer(queries, sliced[0], own_start, offset)
        masked = jnp.where(allowed, scores, NEG)
        new_peak = jnp.maximum(row_peak, jnp.max(masked, axis=-1))
        weights = jnp.where(allowed, jnp.exp(scores - new_peak[..., None]), 0.0)
        return (new_peak, row_total * jnp.exp(row_peak - new_peak) + jnp.sum(weights, axis=-1))

    stats_start = (
        jnp.full((rows_local, H, seq_local), NEG, jnp.float32),
        jnp.zeros((rows_local, H, seq_local), jnp.float32),
    )
    row_peak, row_total = fold_keys(
        stats_step, stats_start, (lax.all_gather(key_rows, "seq", axis=1, tiled=True),)
    )
    logsum = row_peak + jnp.log(row_total)

    def value_step(running, sliced, offset):
        scores, allowed = scorer(queries, sliced[0], own_start, offset)
        prob_block = jnp.where(allowed, jnp.exp(scores - logsum[..., None]), 0.0).astype(
            jnp.bfloat16
        )
        value_four = sliced[1].reshape(rows_local, sliced[1].shape[1], H, HD)
        return running + jnp.einsum(
            "rhqk,rkhd->rqhd", prob_block, value_four, preferred_element_type=jnp.float32
        )

    mixed_four = fold_keys(
        value_step,
        jnp.zeros((rows_local, seq_local, H, HD), jnp.float32),
        (
            lax.all_gather(key_rows, "seq", axis=1, tiled=True),
            lax.all_gather(value_rows, "seq", axis=1, tiled=True),
        ),
    )
    mixed_exact = mixed_four.reshape(flat_count, D)
    mixed_low = mixed_exact.astype(jnp.bfloat16)
    attn_out = jnp.dot(mixed_low, attn_full[3], preferred_element_type=jnp.float32) + bias_o
    hidden, normed_one, inverse_one = norm_forward(inputs + attn_out, gain_one, shift_one)
    ffn_in = hidden.astype(jnp.bfloat16)
    gate_pre = jnp.dot(ffn_in, ffn_full[0], preferred_element_type=jnp.float32) + bias_in
    active = jax.nn.gelu(gate_pre).astype(jnp.bfloat16)
    branch = (
        lax.dot_general(
            active, ffn_full[1], (((1,), (1,)), ((), ())), preferred_element_type=jnp.float32
        )
        + bias_back
    )
    result, normed_two, inverse_two = norm_forward(hidden + branch + inputs, gain_two, shift_two)
    cotangent_live = cotangent_micro.reshape(flat_count, D).astype(jnp.float32) * live_mask
    sum_grad, grad_gain_two, grad_shift_two = norm_backward(
        cotangent_live, normed_two, inverse_two, gain_two
    )
    branch_grad = sum_grad.astype(jnp.bfloat16)
    grad_back = jnp.einsum("td,tf->df", branch_grad, active, preferred_element_type=jnp.float32)
    grad_bias_back = jnp.sum(branch_grad, axis=0, dtype=jnp.float32)
    active_grad = jnp.dot(branch_grad, ffn_full[1], preferred_element_type=jnp.float32)
    gelu_pullback = jax.vjp(jax.nn.gelu, gate_pre)[1]
    gate_grad = gelu_pullback(active_grad)[0].astype(jnp.bfloat16)
    grad_in = jnp.einsum("td,tf->df", ffn_in, gate_grad, preferred_element_type=jnp.float32)
    grad_bias_in = jnp.sum(gate_grad, axis=0, dtype=jnp.float32)
    hidden_grad = sum_grad + lax.dot_general(
        gate_grad, ffn_full[0], (((1,), (1,)), ((), ())), preferred_element_type=jnp.float32
    )
    pre_grad, grad_gain_one, grad_shift_one = norm_backward(
        hidden_grad, normed_one, inverse_one, gain_one
    )
    attn_grad_low = pre_grad.astype(jnp.bfloat16)
    grad_out_weight = jnp.einsum(
        "td,te->de", mixed_low, attn_grad_low, preferred_element_type=jnp.float32
    )
    grad_bias_o = jnp.sum(attn_grad_low, axis=0, dtype=jnp.float32)
    mixed_grad = lax.dot_general(
        attn_grad_low, attn_full[3], (((1,), (1,)), ((), ())), preferred_element_type=jnp.float32
    ).astype(jnp.bfloat16)
    delta = jnp.sum(
        (mixed_grad.astype(jnp.float32) * mixed_exact).reshape(rows_local, seq_local, H, HD),
        axis=-1,
    ).transpose(0, 2, 1)
    query_back = mixed_grad.reshape(rows_local, seq_local, D)
    query_side = (queries, query_back, logsum, delta)
    zero_grad = jnp.zeros((rows_local, seq_local, D), jnp.float32)

    def accumulate(number, carry_state):
        moving_keys, moving_values, key_grad, value_grad, query_grad = carry_state
        owner_index = (own_index - number) % cycle_size
        query_part, key_part, value_part = grad_block(
            scorer, query_side, (moving_keys, moving_values), own_start, owner_index * seq_local
        )
        return (
            moving_keys,
            moving_values,
            key_grad + key_part,
            value_grad + value_part,
            query_grad + query_part,
        )

    def cycle_step(number, carry_state):
        moving_keys, moving_values, key_grad, value_grad, query_grad = accumulate(
            number, carry_state
        )
        key_grad, value_grad = pass_grads(key_grad, value_grad)
        moving_keys, moving_values = from_behind((moving_keys, moving_values), "seq", 1)
        return (moving_keys, moving_values, key_grad, value_grad, query_grad)

    carry_state = lax.fori_loop(
        0, cycle_size - 1, cycle_step, (key_rows, value_rows, zero_grad, zero_grad, zero_grad)
    )
    moving_keys, moving_values, key_grad, value_grad, query_grad = accumulate(
        cycle_size - 1, carry_state
    )
    key_grad, value_grad = pass_grads(key_grad, value_grad)
    query_low = query_grad.reshape(flat_count, D).astype(jnp.bfloat16)
    key_low = key_grad.reshape(flat_count, D).astype(jnp.bfloat16)
    value_low = value_grad.reshape(flat_count, D).astype(jnp.bfloat16)
    stacked = jnp.stack([query_low, key_low, value_low])
    grad_proj = jnp.einsum("td,jte->jde", attn_in, stacked, preferred_element_type=jnp.float32)
    input_grad = (
        pre_grad
        + sum_grad
        + jnp.einsum("jte,jde->td", stacked, attn_full[:3], preferred_element_type=jnp.float32)
    )
    grad_bias_q = jnp.sum(query_low, axis=0, dtype=jnp.float32)
    grad_bias_v = jnp.sum(value_low, axis=0, dtype=jnp.float32)
    row_grads = jnp.sum(input_grad.reshape(rows_local, seq_local, D), axis=1)
    grad_lang = jnp.dot(one_hot.T, row_grads, precision=HIGHEST)
    attn_local = jnp.concatenate([grad_proj, grad_out_weight[None]], axis=0)
    ffn_local = jnp.stack([grad_in, grad_back])
    small_local = jnp.concatenate(
        [
            grad_bias_q,
            grad_bias_v,
            grad_bias_o,
            grad_bias_in,
            grad_bias_back,
            grad_gain_one,
            grad_shift_one,
            grad_gain_two,
            grad_shift_two,
            grad_lang.reshape(-1),
        ]
    )
    output_block = result.reshape(rows_local, seq_local, D).astype(jnp.bfloat16)
    input_block = input_grad.reshape(rows_local, seq_local, D).astype(jnp.bfloat16)
    return (output_block, input_block, (attn_local, ffn_local, small_local))


def shards(
    tokens,
    lengths,
    groups,
    cotangent,
    attn_weights,
    ffn_weights,
    small_params,
    attn_rows,
    attn_cols,
    ffn_rows,
    ffn_cols,
    small_sq,
):
    cycle_size = lax.axis_size("seq")
    own_index = lax.axis_index("seq")
    output_blocks = []
    input_blocks = []
    grad_sums = (
        jnp.zeros_like(attn_weights),
        jnp.zeros_like(ffn_weights),
        jnp.zeros_like(small_params),
    )
    for micro_index in range(tokens.shape[0]):
        full_weights = gather_weights(attn_weights, ffn_weights, small_params)
        output_block, input_block, local_grads = micro_pass(
            tokens[micro_index],
            lengths[micro_index],
            groups[micro_index],
            cotangent[micro_index],
            full_weights,
            cycle_size,
            own_index,
        )
        output_blocks.append(output_block)
        input_blocks.append(input_block)
        shard_grads = scatter_grads(local_grads[0], local_grads[1], local_grads[2])
        grad_sums = tuple(
            (total_part + shard_part for total_part, shard_part in zip(grad_sums, shard_grads))
        )
    attn_grad, ffn_grad, small_grad = grad_sums
    decay = 1.0 - STEP ** (-0.8)
    attn_square = attn_grad * attn_grad + EPS_ONE
    ffn_square = ffn_grad * ffn_grad + EPS_ONE
    attn_rowsum, ffn_rowsum = lax.psum(
        (jnp.sum(attn_square, axis=-1), jnp.sum(ffn_square, axis=-1)), "batch"
    )
    attn_rows_new = decay * attn_rows + (1.0 - decay) * attn_rowsum / D
    ffn_rows_new = decay * ffn_rows + (1.0 - decay) * ffn_rowsum / FF
    attn_colsum, ffn_colsum, attn_rowtotal, ffn_rowtotal = lax.psum(
        (
            jnp.sum(attn_square, axis=1),
            jnp.sum(ffn_square, axis=1),
            jnp.sum(attn_rows_new, axis=-1),
            jnp.sum(ffn_rows_new, axis=-1),
        ),
        "seq",
    )
    attn_cols_new = decay * attn_cols + (1.0 - decay) * attn_colsum / D
    ffn_cols_new = decay * ffn_cols + (1.0 - decay) * ffn_colsum / D
    attn_rel = attn_rows_new / (attn_rowtotal / D)[:, None]
    ffn_rel = ffn_rows_new / (ffn_rowtotal / D)[:, None]
    attn_update = attn_grad * lax.rsqrt(attn_rel[:, :, None] * attn_cols_new[:, None, :])
    ffn_update = ffn_grad * lax.rsqrt(ffn_rel[:, :, None] * ffn_cols_new[:, None, :])
    small_sq_new = decay * small_sq + (1.0 - decay) * (small_grad * small_grad + EPS_ONE)
    small_update = small_grad * lax.rsqrt(small_sq_new)
    squares = lax.psum(
        (
            jnp.sum(attn_update * attn_update, axis=(1, 2)),
            jnp.sum(ffn_update * ffn_update, axis=(1, 2)),
            jnp.sum(small_update * small_update),
            jnp.sum(attn_weights * attn_weights, axis=(1, 2)),
            jnp.sum(ffn_weights * ffn_weights, axis=(1, 2)),
            jnp.sum(small_params * small_params),
        ),
        ("seq", "batch"),
    )
    attn_usq, ffn_usq, small_usq, attn_wsq, ffn_wsq, small_wsq = squares
    attn_scale = jnp.sqrt(attn_wsq / (D * D)) / jnp.maximum(1.0, jnp.sqrt(attn_usq / (D * D)))
    ffn_scale = jnp.sqrt(ffn_wsq / (D * FF)) / jnp.maximum(1.0, jnp.sqrt(ffn_usq / (D * FF)))
    small_scale = jnp.sqrt(small_wsq / NVEC) / jnp.maximum(1.0, jnp.sqrt(small_usq / NVEC))
    attn_new = attn_weights - LEARN * attn_scale[:, None, None] * attn_update
    ffn_new = ffn_weights - LEARN * ffn_scale[:, None, None] * ffn_update
    small_new = small_params - LEARN * small_scale * small_update
    return (
        jnp.stack(output_blocks),
        jnp.stack(input_blocks),
        attn_grad,
        ffn_grad,
        small_grad,
        attn_new,
        ffn_new,
        small_new,
        attn_new.astype(jnp.bfloat16),
        ffn_new.astype(jnp.bfloat16),
        small_new.astype(jnp.bfloat16),
        attn_rows_new,
        attn_cols_new,
        ffn_rows_new,
        ffn_cols_new,
        small_sq_new,
    )


def solution(mesh):
    return jax.shard_map(
        shards,
        mesh=mesh,
        in_specs=(
            P(None, "batch", "seq", None),
            P(None, "batch", None),
            P(None, "batch"),
            P(None, "batch", "seq", None),
            P(None, "seq", "batch"),
            P(None, "seq", "batch"),
            P(("seq", "batch")),
            P(None, "seq"),
            P(None, "batch"),
            P(None, "seq"),
            P(None, "batch"),
            P(("seq", "batch")),
        ),
        out_specs=(
            P(None, "batch", "seq", None),
            P(None, "batch", "seq", None),
            P(None, "seq", "batch"),
            P(None, "seq", "batch"),
            P(("seq", "batch")),
            P(None, "seq", "batch"),
            P(None, "seq", "batch"),
            P(("seq", "batch")),
            P(None, "seq", "batch"),
            P(None, "seq", "batch"),
            P(("seq", "batch")),
            P(None, "seq"),
            P(None, "batch"),
            P(None, "seq"),
            P(None, "batch"),
            P(("seq", "batch")),
        ),
        check_vma=False,
    )
```

profile of v0, /device:TPU:0, one launch (start us, length us, event | category | flops | bytes accessed | tf_op | source)
XLA Modules:
  0.0 1280.8 jit_solution(1424705875626937149)
XLA Ops:
  8.9 6.0 all_gather.40
  18.6 4.9 all-reduce
  23.5 22.4 %all-gather = bf16[16,1,640]{2,1,0:T(2,128)(2,1)S(1)} all-gather(bf16[1,1,640]{2,1,0:T(2,128)(2,1)S(1)} %reshape.2114), channel_id=1, replica_groups=mesh['seq'=16,'batch'=2] {'seq'}, dimensions={0}, use_global_device_ids=true | all-gather | bytes 21760 | tf_op jit(solution)/shard_map/all_gather | solution.py:152
  48.2 10.1 all-gather.8.cloned.1.call-done
  66.9 6.4 all_gather.44
  83.7 17.5 %all-gather.18.cloned.1.call-done = bf16[1,2048,512]{2,1,0:T(8,128)(2,1)} async-done(((bf16[1,128,512]{2,1,0:T(8,128)(2,1)}), bf16[1,2048,512]{2,1,0:T(8,128)(2,1)}) %all-gather.18.cloned.1.call-update) | async-done | bytes 2097168 | tf_op jit(solution)/shard_map/all_gather | solution.py:249
  105.2 14.7 %while.118 = (s32[]{:T(128)}, f32[1,8,128]{2,1,0:T(8,128)S(1)}, f32[1,8,128]{2,1,0:T(8,128)S(1)}, s32[1,128]{1,0:T(1,128)S(1)}, s32[1,2048]{1,0:T(1,128)S(1)}, /...) while((s32[]{:T(128)}, f32[1,8,128]{2,1,0:T(8,128)S(1)}, ...), condition=%wide.region_17.18_spmd.clone, body=%wide.region_14.17_spmd.clone.sunk | while | flops 35264132 | bytes 3174590 | solution.py:99
  119.9 24.3 %all-gather.12.cloned.1.call-done = bf16[1,2048,512]{2,1,0:T(8,128)(2,1)} async-done(((bf16[1,128,512]{2,1,0:T(8,128)(2,1)}), bf16[1,2048,512]{2,1,0:T(8,128)(2,1)}) %all-gather.12.cloned.1.call-update) | async-done | bytes 2097168 | tf_op jit(solution)/shard_map/all_gather | solution.py:249
  148.2 14.7 %while.116 = (s32[]{:T(128)}, f32[1,8,128]{2,1,0:T(8,128)S(1)}, f32[1,8,128]{2,1,0:T(8,128)S(1)}, s32[1,128]{1,0:T(1,128)S(1)}, s32[1,2048]{1,0:T(1,128)S(1)}, /...) while((s32[]{:T(128)}, f32[1,8,128]{2,1,0:T(8,128)S(1)}, ...), condition=%wide.region_5.6_spmd.clone, body=%wide.region_2.5_spmd.clone.sunk | while | flops 35264132 | bytes 3174590 | solution.py:99
  162.9 24.1 %all-gather.16.cloned.1.call-done = bf16[1,2048,512]{2,1,0:T(8,128)(2,1)} async-done(((bf16[1,128,512]{2,1,0:T(8,128)(2,1)}), bf16[1,2048,512]{2,1,0:T(8,128)(2,1)}) %all-gather.16.cloned.1.call-update) | async-done | bytes 2097168 | tf_op jit(solution)/shard_map/all_gather | solution.py:250
  187.0 35.3 %while.119 = (s32[]{:T(128)}, f32[1,128,8,64]{1,3,2,0:T(8,128)}, bf16[1,2048,512]{2,1,0:T(8,128)(2,1)}, s32[1,128]{1,0:T(1,128)S(1)}, s32[1,2048]{1,0:T(1,128)S(...) while((s32[]{:T(128)}, f32[1,128,8,64]{1,3,2,0:T(8,128)}, ...), condition=%wide.region_19.20_spmd.clone, body=%wide.region_18.19_spmd.clone.sunk | while | flops 68420232 | bytes 2830537 | solution.py:99
  223.9 14.6 %all-gather.14.cloned.1.call-done = bf16[2,512,2048]{2,1,0:T(8,128)(2,1)} async-done(((bf16[2,32,2048]{2,1,0:T(8,128)(2,1)}), bf16[2,512,2048]{2,1,0:T(8,128)(2,1)}) %all-gather.14.cloned.1.call-update) | async-done | bytes 4194320 | tf_op jit(solution)/shard_map/all_gather | solution.py:151
  243.7 37.3 %all-gather.10.cloned.1.call-done = bf16[1,2048,512]{2,1,0:T(8,128)(2,1)} async-done(((bf16[1,128,512]{2,1,0:T(8,128)(2,1)}), bf16[1,2048,512]{2,1,0:T(8,128)(2,1)}) %all-gather.10.cloned.1.call-update) | async-done | bytes 2097168 | tf_op jit(solution)/shard_map/all_gather | solution.py:250
  281.0 35.2 %while.117 = (s32[]{:T(128)}, f32[1,128,8,64]{1,3,2,0:T(8,128)}, bf16[1,2048,512]{2,1,0:T(8,128)(2,1)}, s32[1,128]{1,0:T(1,128)S(1)}, s32[1,2048]{1,0:T(1,128)S(...) while((s32[]{:T(128)}, f32[1,128,8,64]{1,3,2,0:T(8,128)}, ...), condition=%wide.region_7.8_spmd.clone, body=%wide.region_6.7_spmd.clone.sunk | while | flops 68420232 | bytes 2830537 | solution.py:99
  338.0 220.3 %while.120 = (s32[]{:T(128)}, bf16[1,128,512]{1,2,0:T(8,128)(2,1)}, bf16[1,128,512]{1,2,0:T(8,128)(2,1)}, f32[1,128,512]{1,2,0:T(8,128)S(1)}, f32[1,128,512]{1,2...) while((s32[]{:T(128)}, bf16[1,128,512]{1,2,0:T(8,128)(2,1)}, ...), condition=%wide.region_30.31_spmd.clone, body=%wide.region_29.30_spmd.clone.sunk | while | flops 85655952 | bytes 9614100 | solution.py:323
  419.7 4.6 collective-permute-done.2
  567.9 207.3 %while.121 = (s32[]{:T(128)}, bf16[1,128,512]{1,2,0:T(8,128)(2,1)S(1)}, bf16[1,128,512]{1,2,0:T(8,128)(2,1)}, f32[1,128,512]{1,2,0:T(8,128)S(1)}, f32[1,128,512]...) while((s32[]{:T(128)}, ...), condition=%wide.region_37.38_spmd.clone, body=%wide.region_36.37_spmd.clone.sunk | while | flops 85655952 | bytes 9614100 | solution.py:323
  573.9 5.5 collective-permute-done.6
  836.9 99.4 %all-reduce.15.cloned.1.call-done = (bf16[4,512,512]{2,0,1:T(4,128)(2,1)}, bf16[4,512,512]{2,0,1:T(4,128)(2,1)}) async-done(((bf16[4,512,512]{2,0,1:T(4,128)(2,1)}, bf16[4,512,512]{2,0,1:T(4,128)(2,1)}), (bf16[4,512,512]{2,0,1:T(4,128)(2,1)}, bf16[4,512,512]{2,0,1:T(4,128)(2,1)})) %all-reduce.15.cloned.1.call-update) | async-done | bytes 4194320
  937.2 7.5 copy.331
  944.7 9.4 reshape.2150
  960.6 7.5 copy.333
  968.1 9.5 reshape.2152
  979.6 32.5 %reduce-scatter.11.cloned.1.call-done = bf16[2,32,2048]{2,1,0:T(8,128)(2,1)} async-done(((bf16[2,512,2048]{2,1,0:T(8,128)(2,1)}), bf16[2,32,2048]{2,1,0:T(8,128)(2,1)}) %reduce-scatter.11.cloned.1.call-update) | async-done | bytes 262160 | tf_op jit(solution)/shard_map/reduce_scatter | solution.py:161
  1019.8 67.7 %reduce-scatter.15.cloned.1.call-done = bf16[2,32,2048]{2,1,0:T(8,128)(2,1)} async-done(((bf16[2,512,2048]{2,1,0:T(8,128)(2,1)}), bf16[2,32,2048]{2,1,0:T(8,128)(2,1)}) %reduce-scatter.15.cloned.1.call-update) | async-done | bytes 262160 | tf_op jit(solution)/shard_map/reduce_scatter | solution.py:161
  1087.6 58.2 %all-reduce.10 = (bf16[10240]{0:T(1024)(128)(2,1)S(1)}, bf16[10240]{0:T(1024)(128)(2,1)S(1)}) all-reduce(bf16[10240]{0:T(1024)(128)(2,1)S(1)} %constant_dynamic-update-slice_fusion.1, bf16[10240]{0:T(1024)(128)(2,1)S(1)} %constant_dynamic-update-slice_fusion), channel_id=12, replica_groups=mesh['seq'=16,'batch'=2] {'seq'}, use_global_device_ids=true, to_apply=%region_68.69.clone | all-reduce | flops 20480 | bytes 81920
  1146.0 4.9 all-reduce.12
  1152.3 5.3 reshape.2151
  1159.4 5.3 reshape.2153
  1167.8 4.9 all-reduce.9
  1173.0 57.6 %all-reduce.8 = (f32[4,256]{1,0:T(4,128)S(1)}, f32[4]{0:T(128)S(1)}, f32[2,1024]{1,0:T(2,128)S(1)}, f32[2]{0:T(128)S(1)}) all-reduce(f32[4,256]{1,0:T(4,128)S(1)} %get-tuple-element.2128, f32[4]{0:T(128)S(1)} %get-tuple-element.2286, f32[2,1024]{1,0:T(2,128)S(1)} %get-tuple-element.2124, ...), channel_id=1, replica_groups=mesh['seq'=16,'batch'=2] {'seq'}, use_global_device_ids=true, to_apply=%region_77.78 | all-reduce | flops 3078 | bytes 24624 | tf_op jit(solution)/shard_map/psum | solution.py:414
  1231.5 37.2 %all-reduce.7 = (f32[4]{0:T(128)S(1)}, f32[4]{0:T(128)S(1)}, f32[2]{0:T(128)S(1)}, f32[2]{0:T(128)S(1)}, f32[]{:T(128)}, /*index=5*/f32[]{:T(128)}) all-reduce(f32[4]{0:T(128)S(1)} %multiply_reduce_fusion.12, f32[4]{0:T(128)S(1)} %copy-done.104, f32[2]{0:T(128)S(1)} %multiply_reduce_fusion, ...), channel_id=1, replica_groups=mesh['seq'=16,'batch'=2] {'seq','batch'}, use_global_device_ids=true, to_apply=%region_79.80 | all-reduce | flops 14 | bytes 112 | tf_op jit(solution)/shard_map/psum | solution.py:431
  (1515 shorter events, 671.8 us)
Async XLA Ops:
  7.2 51.1 %all-gather.8.cloned.1.call-start = ((), (), s32[]{:S(2)}) async-start(), calls=%async_computation.6 | async-start | bytes 2228224 | tf_op jit(solution)/shard_map/all_gather | solution.py:150
  14.9 86.3 %all-gather.18.cloned.1.call-start = ((), (), s32[]{:S(2)}) async-start(), calls=%async_computation.11 | async-start | bytes 2228224 | tf_op jit(solution)/shard_map/all_gather | solution.py:249
  61.0 83.2 %all-gather.12.cloned.1.call-start = ((), (), s32[]{:S(2)}) async-start(), calls=%async_computation.8 | async-start | bytes 2228224 | tf_op jit(solution)/shard_map/all_gather | solution.py:249
  63.8 123.2 %all-gather.16.cloned.1.call-start = ((), (), s32[]{:S(2)}) async-start(), calls=%async_computation.10 | async-start | bytes 2228224 | tf_op jit(solution)/shard_map/all_gather | solution.py:250
  65.1 173.3 %all-gather.14.cloned.1.call-start = ((), (), s32[]{:S(2)}) async-start(), calls=%async_computation.9 | async-start | bytes 4456448 | tf_op jit(solution)/shard_map/all_gather | solution.py:151
  73.4 207.6 %all-gather.10.cloned.1.call-start = ((), (), s32[]{:S(2)}) async-start(), calls=%async_computation.7 | async-start | bytes 2228224 | tf_op jit(solution)/shard_map/all_gather | solution.py:250
  81.5 854.7 %all-reduce.15.cloned.1.call-start = ((), (), s32[]{:S(2)}) async-start(), calls=%async_computation.18 | async-start | bytes 8388608
  339.1 14.4 %collective-permute-start = (bf16[1,128,512]{1,2,0:T(8,128)(2,1)S(1)}, bf16[1,128,512]{1,2,0:T(8,128)(2,1)}, u32[]{:S(2)}, u32[]{:S(2)}) collective-permute-start(bf16[1,128,512]{1,2,0:T(8,128)(2,1)S(1)} %copy.401), channel_id=1, source_target_pairs={{30,0},{0,2},{2,4},{4,6},{6,8},{8,10},{10,12},{12,14},{14,16},{16,... | collective-permute-start | bytes 393224 | tf_op jit(solution)/shard_map/while/body/eval_jaxpr/ppermute | solution.py:30
  530.0 13.7 %collective-permute-start = (bf16[1,128,512]{1,2,0:T(8,128)(2,1)S(1)}, bf16[1,128,512]{1,2,0:T(8,128)(2,1)}, u32[]{:S(2)}, u32[]{:S(2)}) collective-permute-start(bf16[1,128,512]{1,2,0:T(8,128)(2,1)S(1)} %copy.401), channel_id=1, source_target_pairs={{30,0},{0,2},{2,4},{4,6},{6,8},{8,10},{10,12},{12,14},{14,16},{16,... | collective-permute-start | bytes 393224 | tf_op jit(solution)/shard_map/while/body/eval_jaxpr/ppermute | solution.py:30
  567.9 13.8 %collective-permute-start.4 = (bf16[1,128,512]{1,2,0:T(8,128)(2,1)S(1)}, bf16[1,128,512]{1,2,0:T(8,128)(2,1)S(1)}, u32[]{:S(2)}, u32[]{:S(2)}) collective-permute-start(bf16[1,128,512]{1,2,0:T(8,128)(2,1)S(1)} %copy.383), channel_id=1, source_target_pairs={{30,0},{0,2},{2,4},{4,6},{6,8},{8,10},{10,12},{12,14},{14,16},{16,... | collective-permute-start | bytes 393224 | tf_op jit(solution)/shard_map/while/body/eval_jaxpr/ppermute | solution.py:30
  581.8 13.8 %collective-permute-start.4 = (bf16[1,128,512]{1,2,0:T(8,128)(2,1)S(1)}, bf16[1,128,512]{1,2,0:T(8,128)(2,1)S(1)}, u32[]{:S(2)}, u32[]{:S(2)}) collective-permute-start(bf16[1,128,512]{1,2,0:T(8,128)(2,1)S(1)} %copy.383), channel_id=1, source_target_pairs={{30,0},{0,2},{2,4},{4,6},{6,8},{8,10},{10,12},{12,14},{14,16},{16,... | collective-permute-start | bytes 393224 | tf_op jit(solution)/shard_map/while/body/eval_jaxpr/ppermute | solution.py:30
  595.6 13.8 %collective-permute-start.4 = (bf16[1,128,512]{1,2,0:T(8,128)(2,1)S(1)}, bf16[1,128,512]{1,2,0:T(8,128)(2,1)S(1)}, u32[]{:S(2)}, u32[]{:S(2)}) collective-permute-start(bf16[1,128,512]{1,2,0:T(8,128)(2,1)S(1)} %copy.383), channel_id=1, source_target_pairs={{30,0},{0,2},{2,4},{4,6},{6,8},{8,10},{10,12},{12,14},{14,16},{16,... | collective-permute-start | bytes 393224 | tf_op jit(solution)/shard_map/while/body/eval_jaxpr/ppermute | solution.py:30
  609.4 13.8 %collective-permute-start.4 = (bf16[1,128,512]{1,2,0:T(8,128)(2,1)S(1)}, bf16[1,128,512]{1,2,0:T(8,128)(2,1)S(1)}, u32[]{:S(2)}, u32[]{:S(2)}) collective-permute-start(bf16[1,128,512]{1,2,0:T(8,128)(2,1)S(1)} %copy.383), channel_id=1, source_target_pairs={{30,0},{0,2},{2,4},{4,6},{6,8},{8,10},{10,12},{12,14},{14,16},{16,... | collective-permute-start | bytes 393224 | tf_op jit(solution)/shard_map/while/body/eval_jaxpr/ppermute | solution.py:30
  623.2 13.8 %collective-permute-start.4 = (bf16[1,128,512]{1,2,0:T(8,128)(2,1)S(1)}, bf16[1,128,512]{1,2,0:T(8,128)(2,1)S(1)}, u32[]{:S(2)}, u32[]{:S(2)}) collective-permute-start(bf16[1,128,512]{1,2,0:T(8,128)(2,1)S(1)} %copy.383), channel_id=1, source_target_pairs={{30,0},{0,2},{2,4},{4,6},{6,8},{8,10},{10,12},{12,14},{14,16},{16,... | collective-permute-start | bytes 393224 | tf_op jit(solution)/shard_map/while/body/eval_jaxpr/ppermute | solution.py:30
  637.0 13.8 %collective-permute-start.4 = (bf16[1,128,512]{1,2,0:T(8,128)(2,1)S(1)}, bf16[1,128,512]{1,2,0:T(8,128)(2,1)S(1)}, u32[]{:S(2)}, u32[]{:S(2)}) collective-permute-start(bf16[1,128,512]{1,2,0:T(8,128)(2,1)S(1)} %copy.383), channel_id=1, source_target_pairs={{30,0},{0,2},{2,4},{4,6},{6,8},{8,10},{10,12},{12,14},{14,16},{16,... | collective-permute-start | bytes 393224 | tf_op jit(solution)/shard_map/while/body/eval_jaxpr/ppermute | solution.py:30
  650.9 13.8 %collective-permute-start.4 = (bf16[1,128,512]{1,2,0:T(8,128)(2,1)S(1)}, bf16[1,128,512]{1,2,0:T(8,128)(2,1)S(1)}, u32[]{:S(2)}, u32[]{:S(2)}) collective-permute-start(bf16[1,128,512]{1,2,0:T(8,128)(2,1)S(1)} %copy.383), channel_id=1, source_target_pairs={{30,0},{0,2},{2,4},{4,6},{6,8},{8,10},{10,12},{12,14},{14,16},{16,... | collective-permute-start | bytes 393224 | tf_op jit(solution)/shard_map/while/body/eval_jaxpr/ppermute | solution.py:30
  664.7 13.8 %collective-permute-start.4 = (bf16[1,128,512]{1,2,0:T(8,128)(2,1)S(1)}, bf16[1,128,512]{1,2,0:T(8,128)(2,1)S(1)}, u32[]{:S(2)}, u32[]{:S(2)}) collective-permute-start(bf16[1,128,512]{1,2,0:T(8,128)(2,1)S(1)} %copy.383), channel_id=1, source_target_pairs={{30,0},{0,2},{2,4},{4,6},{6,8},{8,10},{10,12},{12,14},{14,16},{16,... | collective-permute-start | bytes 393224 | tf_op jit(solution)/shard_map/while/body/eval_jaxpr/ppermute | solution.py:30
  678.5 13.8 %collective-permute-start.4 = (bf16[1,128,512]{1,2,0:T(8,128)(2,1)S(1)}, bf16[1,128,512]{1,2,0:T(8,128)(2,1)S(1)}, u32[]{:S(2)}, u32[]{:S(2)}) collective-permute-start(bf16[1,128,512]{1,2,0:T(8,128)(2,1)S(1)} %copy.383), channel_id=1, source_target_pairs={{30,0},{0,2},{2,4},{4,6},{6,8},{8,10},{10,12},{12,14},{14,16},{16,... | collective-permute-start | bytes 393224 | tf_op jit(solution)/shard_map/while/body/eval_jaxpr/ppermute | solution.py:30
  692.3 13.8 %collective-permute-start.4 = (bf16[1,128,512]{1,2,0:T(8,128)(2,1)S(1)}, bf16[1,128,512]{1,2,0:T(8,128)(2,1)S(1)}, u32[]{:S(2)}, u32[]{:S(2)}) collective-permute-start(bf16[1,128,512]{1,2,0:T(8,128)(2,1)S(1)} %copy.383), channel_id=1, source_target_pairs={{30,0},{0,2},{2,4},{4,6},{6,8},{8,10},{10,12},{12,14},{14,16},{16,... | collective-permute-start | bytes 393224 | tf_op jit(solution)/shard_map/while/body/eval_jaxpr/ppermute | solution.py:30
  706.2 13.8 %collective-permute-start.4 = (bf16[1,128,512]{1,2,0:T(8,128)(2,1)S(1)}, bf16[1,128,512]{1,2,0:T(8,128)(2,1)S(1)}, u32[]{:S(2)}, u32[]{:S(2)}) collective-permute-start(bf16[1,128,512]{1,2,0:T(8,128)(2,1)S(1)} %copy.383), channel_id=1, source_target_pairs={{30,0},{0,2},{2,4},{4,6},{6,8},{8,10},{10,12},{12,14},{14,16},{16,... | collective-permute-start | bytes 393224 | tf_op jit(solution)/shard_map/while/body/eval_jaxpr/ppermute | solution.py:30
  720.0 13.8 %collective-permute-start.4 = (bf16[1,128,512]{1,2,0:T(8,128)(2,1)S(1)}, bf16[1,128,512]{1,2,0:T(8,128)(2,1)S(1)}, u32[]{:S(2)}, u32[]{:S(2)}) collective-permute-start(bf16[1,128,512]{1,2,0:T(8,128)(2,1)S(1)} %copy.383), channel_id=1, source_target_pairs={{30,0},{0,2},{2,4},{4,6},{6,8},{8,10},{10,12},{12,14},{14,16},{16,... | collective-permute-start | bytes 393224 | tf_op jit(solution)/shard_map/while/body/eval_jaxpr/ppermute | solution.py:30
  733.8 13.8 %collective-permute-start.4 = (bf16[1,128,512]{1,2,0:T(8,128)(2,1)S(1)}, bf16[1,128,512]{1,2,0:T(8,128)(2,1)S(1)}, u32[]{:S(2)}, u32[]{:S(2)}) collective-permute-start(bf16[1,128,512]{1,2,0:T(8,128)(2,1)S(1)} %copy.383), channel_id=1, source_target_pairs={{30,0},{0,2},{2,4},{4,6},{6,8},{8,10},{10,12},{12,14},{14,16},{16,... | collective-permute-start | bytes 393224 | tf_op jit(solution)/shard_map/while/body/eval_jaxpr/ppermute | solution.py:30
  747.6 13.8 %collective-permute-start.4 = (bf16[1,128,512]{1,2,0:T(8,128)(2,1)S(1)}, bf16[1,128,512]{1,2,0:T(8,128)(2,1)S(1)}, u32[]{:S(2)}, u32[]{:S(2)}) collective-permute-start(bf16[1,128,512]{1,2,0:T(8,128)(2,1)S(1)} %copy.383), channel_id=1, source_target_pairs={{30,0},{0,2},{2,4},{4,6},{6,8},{8,10},{10,12},{12,14},{14,16},{16,... | collective-permute-start | bytes 393224 | tf_op jit(solution)/shard_map/while/body/eval_jaxpr/ppermute | solution.py:30
  761.4 13.8 %collective-permute-start.4 = (bf16[1,128,512]{1,2,0:T(8,128)(2,1)S(1)}, bf16[1,128,512]{1,2,0:T(8,128)(2,1)S(1)}, u32[]{:S(2)}, u32[]{:S(2)}) collective-permute-start(bf16[1,128,512]{1,2,0:T(8,128)(2,1)S(1)} %copy.383), channel_id=1, source_target_pairs={{30,0},{0,2},{2,4},{4,6},{6,8},{8,10},{10,12},{12,14},{14,16},{16,... | collective-permute-start | bytes 393224 | tf_op jit(solution)/shard_map/while/body/eval_jaxpr/ppermute | solution.py:30
  789.2 17.7 %collective-permute-start.9 = (bf16[1,128,512]{2,1,0:T(8,128)(2,1)}, bf16[1,128,512]{2,1,0:T(8,128)(2,1)}, u32[]{:S(2)}, u32[]{:S(2)}) collective-permute-start(bf16[1,128,512]{2,1,0:T(8,128)(2,1)} %add_convert_fusion.4), channel_id=1, source_target_pairs={{30,0},{0,2},{2,4},{4,6},{6,8},{8,10},{10,12},{12,14},{14,16},{16,... | collective-permute-start | bytes 393224 | tf_op jit(solution)/shard_map/ppermute | solution.py:30
  798.8 15.7 %collective-permute-start.11 = (bf16[1,128,512]{2,1,0:T(8,128)(2,1)}, bf16[1,128,512]{2,1,0:T(8,128)(2,1)}, u32[]{:S(2)}, u32[]{:S(2)}) collective-permute-start(bf16[1,128,512]{2,1,0:T(8,128)(2,1)} %add_convert_fusion), channel_id=1, source_target_pairs={{30,0},{0,2},{2,4},{4,6},{6,8},{8,10},{10,12},{12,14},{14,16},{16,... | collective-permute-start | bytes 393224 | tf_op jit(solution)/shard_map/ppermute | solution.py:30
  822.3 189.9 %reduce-scatter.11.cloned.1.call-start = ((), (), s32[]{:S(2)}) async-start(), calls=%async_computation.12 | async-start | bytes 4456448 | tf_op jit(solution)/shard_map/reduce_scatter | solution.py:161
  828.3 259.3 %reduce-scatter.15.cloned.1.call-start = ((), (), s32[]{:S(2)}) async-start(), calls=%async_computation.14 | async-start | bytes 4456448 | tf_op jit(solution)/shard_map/reduce_scatter | solution.py:161
  834.4 317.9 %reduce-scatter.19.cloned.1.call-start = ((), (), s32[]{:S(2)}) async-start(), calls=%async_computation.16 | async-start | bytes 196608
  954.1 205.3 %reduce-scatter.21.cloned.1.call-start = ((), (), s32[]{:S(2)}) async-start(), calls=%async_computation.17 | async-start | bytes 196608
  977.6 189.1 %reduce-scatter.13.cloned.1.call-start = ((), (), s32[]{:S(2)}) async-start(), calls=%async_computation.13 | async-start | bytes 393216 | tf_op jit(solution)/shard_map/reduce_scatter | solution.py:172
  1012.2 154.5 %reduce-scatter.17.cloned.1.call-start = ((), (), s32[]{:S(2)}) async-start(), calls=%async_computation.15 | async-start | bytes 393216 | tf_op jit(solution)/shard_map/reduce_scatter | solution.py:172
  (221 other events, 4955.4 us)
Sparse Core Ops, SparseCore 0:
  15.0 43.2 all-gather.7
  61.1 40.0 all-gather.17
  104.0 40.1 all-gather.11
  146.8 40.1 all-gather.15
  189.0 49.3 all-gather.13
  241.0 39.8 all-gather.9
  822.4 113.8 all-reduce.14
  940.6 71.4 reduce-scatter.10
  1016.0 71.5 reduce-scatter.14
  1090.3 9.2 reduce-scatter.18
  1102.4 10.2 reduce-scatter.20
  1114.9 11.6 reduce-scatter.12
  1128.8 11.6 reduce-scatter.16
where the time goes:
time: 1290 us; the launch traced here: 1280 us
  waiting for transfers between devices  478 us (37%)
  other arithmetic  223 us (17%)
  blocking collectives  203 us (16%)
  local copies, waits for them, and re-layouts  198 us (15%)
  matrix products  149 us (12%)
  between operations  20 us (2%)
    ppermute x124, waiting for transfers between devices, from_behind(): return lax.ppermute(block, axis, route)  150 us
    reduce_scatter x2, waiting for transfers between devices, scatter_grads(): lax.psum_scatter(ffn_part.astype(jnp.bfloat16), 'seq', scatter_dimension=...  100 us
    unnamed x16, waiting for transfers between devices  99.6 us
    unnamed x283, local copies, waits for them, and re-layouts  76.4 us
    unnamed x3, blocking collectives  68.1 us
    all_gather x2, waiting for transfers between devices, micro_pass(): lax.all_gather(value_rows, 'seq', axis=1, tiled=True)  61.3 us
    psum x1, blocking collectives, shards(): lax.psum((jnp.sum(attn_square, axis=1), jnp.sum(ffn_square, axis=1), jnp....  57.6 us
    convert_element_type x64, other arithmetic, shortened(): a.astype(jnp.bfloat16)  49.3 us
  transfers between devices with their start and end apart: 137, of which 69 were waited for; matrix products, arithmetic and copies ran while one was open for 36% of the time, Pallas kernels for 0%

commit v1 on v0

v1 whole, which is shorter than its diff:
```python
import functools

import jax
import jax.numpy as jnp
from jax import lax
from jax.experimental import pallas as pl
from jax.experimental.pallas import tpu as pltpu
from jax.sharding import PartitionSpec as P

D = 512
H = 8
HD = 64
FF = 2048
GROUPS = 8
SEGS = 64
STEP = 10
NVEC = 10240
LANES = 128

NEG = -1e30
EPS = 1e-05
EPS_ONE = 1e-30
LEARN = 1.0
DECAY = 1.0 - STEP ** (-0.8)
SCALE = HD ** (-0.5)
LOG2E = 1.4426950408889634
FRAMES = 16
FRAME_ROWS = NVEC // FRAMES // LANES
GROUP = 4
BF = jnp.bfloat16
F32 = jnp.float32
VMEM_SPEC = pl.BlockSpec(memory_space=pltpu.VMEM)
SMEM_SPEC = pl.BlockSpec(memory_space=pltpu.SMEM)

ROW_BQ, ROW_BV, ROW_BO, ROW_B1, ROW_B2 = 0, 4, 8, 12, 28
ROW_G1, ROW_S1, ROW_G2, ROW_S2, ROW_E = 32, 36, 40, 44, 48


def mm(a, b):
    return lax.dot_general(a, b, (((1,), (0,)), ((), ())), preferred_element_type=F32)


def mm_nt(a, b):
    return lax.dot_general(a, b, (((1,), (1,)), ((), ())), preferred_element_type=F32)


def mm_tn(a, b):
    return lax.dot_general(a, b, (((0,), (0,)), ((), ())), preferred_element_type=F32)


def small_piece(small_ref, row, count):
    parts = [small_ref[r // FRAME_ROWS, pl.ds(r % FRAME_ROWS, 1), :] for r in range(row, row + count)]
    return jnp.concatenate(parts, axis=1)


def add_small(ref, row, values):
    for k in range(values.shape[1] // LANES):
        r = row + k
        ref[r // FRAME_ROWS, pl.ds(r % FRAME_ROWS, 1), :] += values[:, k * LANES : (k + 1) * LANES]


def low_half():
    return lax.broadcasted_iota(jnp.int32, (1, LANES), 1) < HD


def swap_halves(x):
    return pltpu.roll(x, HD, 1)


def heads_to_rows(tiles):
    low = low_half()
    first, second = [], []
    for j in range(H // 2):
        a, b = tiles[2 * j], tiles[2 * j + 1]
        first.append(jnp.where(low, a, swap_halves(b)))
        second.append(jnp.where(low, swap_halves(a), b))
    return jnp.concatenate(first, axis=1), jnp.concatenate(second, axis=1)


def rows_to_heads(first, second):
    low = low_half()
    tiles = []
    for j in range(H // 2):
        a = first[:, j * LANES : (j + 1) * LANES]
        b = second[:, j * LANES : (j + 1) * LANES]
        tiles.append(jnp.where(low, a, swap_halves(b)))
        tiles.append(jnp.where(low, swap_halves(a), b))
    return tiles


def wrap(value, count):
    return value - jnp.where(value >= count, count, 0)


def outwards(count):
    return sorted(range(1, count), key=lambda k: (abs(2 * k - count), k))


class Place:
    def __init__(self):
        self.n_s, self.n_b = lax.axis_size("seq"), lax.axis_size("batch")
        self.s, self.b = lax.axis_index("seq"), lax.axis_index("batch")
        self.n_z, self.parts = self.n_s // 4, self.n_s // H
        self.z, self.xc = self.s // 4, self.s % 4
        self.x, self.c = self.xc // 2, self.xc % 2
        self.other_x = (1 - self.x) * 2 + self.c
        self.other_c = self.x * 2 + 1 - self.c
        self.h, self.g = self.s // self.parts, self.s % self.parts
        self.z_ahead = [wrap(self.z + k, self.n_z) for k in range(self.n_z)]
        self.b_ahead = [wrap(self.b + k, self.n_b) for k in range(self.n_b)]
        self.xc_ahead = [wrap(self.xc + k, 4) for k in range(4)]
        self.h_ahead = [wrap(self.h + k, H) for k in range(H)]
        self.g_ahead = [wrap(self.g + k, self.parts) for k in range(self.parts)]
        self.at_z = [z * 4 + self.xc for z in self.z_ahead]
        self.at_x, self.at_core = self.z * 4 + self.other_x, self.z * 4 + self.other_c
        self.at_head = [h * self.parts + self.g for h in self.h_ahead]
        self.at_part = [self.h * self.parts + g for g in self.g_ahead]

    def along_z(self, k):
        return (self.at_z[k], self.b)

    def across_x(self):
        return (self.at_x, self.b)

    def across_core(self):
        return (self.at_core, self.b)

    def batch_ahead(self, k):
        return self.b_ahead[k]

    def batch_behind(self, k):
        return self.b_ahead[(self.n_b - k) % self.n_b]

    def across_batch(self, k):
        return (self.s, self.b_ahead[k])

    def head_ahead(self, k):
        return self.h_ahead[k % H] if isinstance(k, int) else wrap(self.h + k, H)

    def head_behind(self, k):
        return self.h_ahead[(H - k) % H] if isinstance(k, int) else wrap(self.h + H - k, H)

    def across_heads(self, k):
        return (self.at_head[k] if isinstance(k, int) else self.head_ahead(k) * self.parts + self.g, self.b)

    def part_ahead(self, k):
        return self.g_ahead[k]

    def across_parts(self, k):
        return (self.at_part[k], self.b)


def greet(peers):
    barrier = pltpu.get_barrier_semaphore()
    for peer in peers:
        pl.semaphore_signal(barrier, inc=1, device_id=peer, device_id_type=pl.DeviceIdType.MESH)
    pl.semaphore_wait(barrier, len(peers))


def greet_all(place):
    barrier = pltpu.get_barrier_semaphore()

    def hello(b, i, carry):
        peer = (wrap(place.s + i, place.n_s), b)
        pl.semaphore_signal(barrier, inc=1, device_id=peer, device_id_type=pl.DeviceIdType.MESH)
        return carry

    for k, b in enumerate(place.b_ahead):
        lax.fori_loop(0 if k else 1, place.n_s, functools.partial(hello, b), 0)
    pl.semaphore_wait(barrier, place.n_s * place.n_b - 1)


def far_first(i):
    if isinstance(i, int) and i in (0, H):
        return i
    return H // 2 + i // 2 * (1 - i % 2 * 2)


class Copy:
    def __init__(self, wire, i, build):
        self.wire, self.i, self.build = wire, i, build

    def made(self):
        return self.wire.make(self.i, *self.build())

    def start(self):
        self.made().start()

    def wait_recv(self):
        self.made().wait_recv()

    def wait_send(self):
        self.made().wait_send()


class Wire:
    def __init__(self, send_sems, recv_sems):
        self.send_sems, self.recv_sems, self.copies, self.used = send_sems, recv_sems, [], 0

    def reserve(self, count):
        self.used += count
        return self.used - count

    def make(self, i, src, dst, peer):
        return pltpu.make_async_remote_copy(
            src_ref=src,
            dst_ref=dst,
            send_sem=self.send_sems.at[i],
            recv_sem=self.recv_sems.at[i],
            device_id=peer,
            device_id_type=pl.DeviceIdType.MESH,
        )

    def plan(self, build):
        return Copy(self, self.reserve(1), build)

    def send(self, build):
        copy = self.plan(build)
        copy.start()
        self.copies.append(copy)
        return copy

    def drain(self):
        for copy in self.copies:
            copy.wait_send()
        self.copies = []


def received(copies):
    for copy in copies:
        copy.wait_recv()


class Gather:
    def __init__(self, place, wire, src, dst, own_sem, cut):
        self.place, self.wire, self.src, self.dst, self.cut, self.own_sem = place, wire, src, dst, cut, own_sem
        self.own().start()
        self.along = [wire.send(lambda k=k: (src, self.slot(place.z), place.along_z(k))) for k in range(1, place.n_z)]

    def slot(self, z):
        return self.dst.at[self.place.b, :, z, self.place.xc]

    def own(self):
        return pltpu.make_async_copy(self.src, self.slot(self.place.z), self.own_sem)

    def forward(self, part, *peers):
        return [self.wire.send(lambda peer=peer: (part(), part(), peer())) for peer in peers]

    def column(self, b, xc):
        return lambda: self.dst.at[b(), :, :, xc]

    def half(self, b, xc, second):
        span = pl.ds(self.cut, self.place.n_z - self.cut) if second else pl.ds(0, self.cut)
        return lambda: self.dst.at[b(), :, span, xc]

    def batch_peers(self):
        return [lambda k=k: self.place.across_batch(k) for k in range(1, self.place.n_b)]

    def to_plane(self):
        p = self.place
        self.own().wait()
        received(self.along)
        peers = [p.across_x, p.across_core] + self.batch_peers()
        self.plane = self.forward(self.column(lambda: p.b, p.xc), *peers)

    def to_diagonal(self):
        p = self.place
        self.plane[0].wait_recv()
        self.diagonal = self.forward(self.half(lambda: p.b, p.other_x, 0), *self.batch_peers())
        self.cores = [self.plane[1]] + self.forward(self.column(lambda: p.b, p.other_x), p.across_core)
        for k in range(1, p.n_b):
            b = lambda k=k: p.batch_behind(k)
            self.plane[1 + k].wait_recv()
            self.diagonal += self.forward(self.half(b, p.xc, 1), p.across_x)
            self.cores += self.forward(self.column(b, p.xc), p.across_core)

    def to_cores(self):
        p = self.place
        for k in range(1, p.n_b):
            for second in range(2):
                self.diagonal[(p.n_b - 1) * second + k - 1].wait_recv()
                part = self.half(lambda k=k: p.batch_behind(k), p.other_x, second)
                self.cores += self.forward(part, p.across_core)

    def finish(self):
        received(self.cores)


class ShortGather(Gather):
    def to_plane(self):
        p = self.place
        self.own().wait()
        received(self.along)
        diagonal = [
            lambda k=k: (p.z * 4 + p.other_x, p.batch_ahead(k)) for k in range(1, p.n_b)
        ]
        peers = [p.across_core, p.across_x] + self.batch_peers() + diagonal
        self.plane = self.forward(self.column(lambda: p.b, p.xc), *peers)

    def to_cores(self):
        p = self.place
        behind = [lambda k=k: p.batch_behind(k) for k in range(1, p.n_b)]
        columns = [(lambda: p.b, p.other_x)] + [(b, p.xc) for b in behind] + [(b, p.other_x) for b in behind]
        self.cores = [self.plane[0]]
        for copy, (b, xc) in zip(self.plane[1:], columns):
            copy.wait_recv()
            self.cores += self.forward(self.column(b, xc), p.across_core)


def normed_of(values):
    center = values - jnp.mean(values, axis=-1, keepdims=True)
    inverse = lax.rsqrt(jnp.mean(center * center, axis=-1, keepdims=True) + EPS)
    return center * inverse, inverse


def norm_back(grad_norm, normed, inverse):
    return inverse * (
        grad_norm
        - jnp.mean(grad_norm, axis=-1, keepdims=True)
        - normed * jnp.mean(grad_norm * normed, axis=-1, keepdims=True)
    )


def gelu_pair(z):
    c = 0.7978845608028654
    z2 = z * z
    t = jnp.tanh(c * z * (1.0 + 0.044715 * z2))
    half = 0.5 * (1.0 + t)
    slope = half + 0.5 * z * (1.0 - t * t) * (c * (1.0 + 3 * 0.044715 * z2))
    return z * half, slope


def language_rows(groups_ref, small_ref, rows):
    table = [small_piece(small_ref, ROW_E + 4 * e, 4) for e in range(GROUPS)]
    out = []
    for m in range(rows):
        acc = jnp.zeros_like(table[0])
        for e in range(GROUPS):
            acc = acc + jnp.where(groups_ref[m] == e, table[e], 0.0)
        out.append(acc)
    return out


def column_sum(x):
    return jnp.sum(x, axis=0, keepdims=True)


class Scatter:
    def __init__(self, place, wire, part, core, acc, far, near, plane_x, plane_b, column):
        self.begin(place, wire, part, core, acc, column)
        self.far, self.near, self.plane_x, self.plane_b = far, near, plane_x, plane_b
        self.cut = far.shape[2]

    def begin(self, place, wire, part, core, acc, column):
        self.place, self.wire = place, wire
        self.part, self.core, self.acc, self.column = part, core, acc, column
        self.kind = part.dtype
        self.x, self.c = place.x, place.c
        self.slabs = part.shape[1]

    def add(self, target, *others):
        total = target[...].astype(F32)
        for other in others:
            total = total + other[...].astype(F32)
        target[...] = total.astype(self.kind)

    def each(self, body, first=0, last=None):
        for j in range(self.slabs):

            def step(z, carry, j=j):
                body(j, z)
                return carry

            lax.fori_loop(first, self.place.n_z if last is None else last, step, 0)

    def to_core(self):
        p = self.place
        self.moved = [self.wire.send(lambda: (self.part.at[:, :, :, :, 1 - self.c], self.core, p.across_core()))]

    def join(self):
        p = self.place
        received(self.moved)
        for j in range(self.slabs):

            def body(b, carry, j=j):
                def at_z(z, carry):
                    for x in range(2):
                        total = self.part[b, j, z, x, self.c].astype(F32) + self.core[b, j, z, x].astype(F32)
                        self.acc[b, j, z, x] = total.astype(self.kind)
                    return carry

                return lax.fori_loop(0, p.n_z, at_z, carry)

            lax.fori_loop(0, p.n_b, body, 0)

    def to_diagonal(self):
        p = self.place
        self.join()
        cut, rest = pl.ds(0, self.cut), pl.ds(self.cut, p.n_z - self.cut)
        self.moved_far, self.moved_near = [], []
        for k in range(1, p.n_b):
            diagonal = lambda k=k: self.acc.at[p.batch_ahead(k), :, :, 1 - self.x]
            self.moved_far.append(
                self.wire.send(
                    lambda k=k, part=diagonal: (part().at[:, cut], self.far.at[k - 1], p.across_batch(k))
                )
            )
            self.moved_near.append(
                self.wire.send(lambda k=k, part=diagonal: (part().at[:, rest], self.near.at[k - 1], p.across_x()))
            )

    def to_plane(self):
        p = self.place
        for k in range(1, p.n_b):
            self.moved_near[k - 1].wait_recv()
            self.each(
                lambda j, z, k=k: self.add(
                    self.acc.at[p.batch_ahead(k), j, z, self.x], self.near.at[k - 1, j, z - self.cut]
                ),
                self.cut,
            )
        received(self.moved_far)
        self.each(
            lambda j, z: self.add(
                self.acc.at[p.b, j, z, 1 - self.x], *[self.far.at[k - 1, j, z] for k in range(1, p.n_b)]
            ),
            0,
            self.cut,
        )
        self.moved = [self.wire.send(lambda: (self.acc.at[p.b, :, :, 1 - self.x], self.plane_x, p.across_x()))]
        self.moved += [
            self.wire.send(
                lambda k=k: (
                    self.acc.at[p.batch_ahead(k), :, :, self.x],
                    self.plane_b.at[k - 1],
                    p.across_batch(k),
                )
            )
            for k in range(1, p.n_b)
        ]

    def others(self, j, z):
        return [self.plane_x.at[j, z]] + [self.plane_b.at[k - 1, j, z] for k in range(1, self.place.n_b)]

    def to_owner(self):
        p = self.place
        received(self.moved)
        self.each(lambda j, z: self.add(self.acc.at[p.b, j, z, self.x], *self.others(j, z)))
        self.moved = [
            self.wire.send(
                lambda k=k: (
                    self.acc.at[p.b, :, p.z_ahead[k], self.x],
                    self.column.at[k - 1],
                    p.along_z(k),
                )
            )
            for k in range(1, p.n_z)
        ]

    def total(self, j):
        p = self.place
        out = self.acc[p.b, j, p.z, self.x].astype(F32)
        for k in range(1, p.n_z):
            out = out + self.column[k - 1, j].astype(F32)
        return out

    def finish(self):
        received(self.moved)


class ShortScatter(Scatter):
    def __init__(self, place, wire, part, core, acc, plane, column):
        self.begin(place, wire, part, core, acc, column)
        self.plane = plane

    def to_plane(self):
        p = self.place
        self.join()
        self.moved = []
        for k in range(p.n_b):
            for dx in range(2):
                if k or dx:

                    def build(k=k, dx=dx, slot=len(self.moved)):
                        x = self.x if dx == 0 else 1 - self.x
                        to = p.z * 4 + (p.other_x if dx else p.xc)
                        b = p.batch_ahead(k)
                        return (self.acc.at[b, :, :, x], self.plane.at[slot], (to, b))

                    self.moved.append(self.wire.send(build))

    def others(self, j, z):
        return [self.plane.at[k, j, z] for k in range(2 * self.place.n_b - 1)]


def short_scratch(n_b, slabs, n_z, r, cols, kind):
    return [
        pltpu.VMEM((n_b, slabs, n_z, 2, r, cols), kind),
        pltpu.VMEM((n_b, slabs, n_z, 2, r, cols), kind),
        pltpu.VMEM((2 * n_b - 1, slabs, n_z, r, cols), kind),
        pltpu.VMEM((n_z - 1, slabs, r, cols), kind),
    ]


def scatter_scratch(n_b, slabs, n_z, r, cols, kind):
    return [
        pltpu.VMEM((n_b, slabs, n_z, 2, r, cols), kind),
        pltpu.VMEM((n_b, slabs, n_z, 2, r, cols), kind),
        pltpu.VMEM((n_b - 1, slabs, n_z - n_z // 4, r, cols), kind),
        pltpu.VMEM((n_b - 1, slabs, n_z // 4, r, cols), kind),
        pltpu.VMEM((slabs, n_z, r, cols), kind),
        pltpu.VMEM((n_b - 1, slabs, n_z, r, cols), kind),
        pltpu.VMEM((n_z - 1, slabs, r, cols), kind),
    ]


SCATTER_SCRATCH, SHORT_SCRATCH = 7, 4
SLABS = 6


def lanes_of(values):
    lane = lax.broadcasted_iota(jnp.int32, (8, LANES), 1)
    row = lax.broadcasted_iota(jnp.int32, (8, LANES), 0)
    tile = jnp.zeros((8, LANES), F32)
    for j, value in enumerate(values):
        if value is not None:
            tile = tile + jnp.where((lane == j) & (row == 0), value, 0.0)
    return tile


def sum_all(x):
    return jnp.sum(jnp.sum(x, axis=1, keepdims=True), axis=0, keepdims=True)


def to_frame(values, at):
    wide = jnp.concatenate([values, jnp.zeros((1, 8 * LANES - values.shape[1]), F32)], axis=1)
    wide = pltpu.roll(wide, at, 1)
    return jnp.concatenate([wide[:, k * LANES : (k + 1) * LANES] for k in range(8)], axis=0)


def from_frame(tile, at, chunk):
    wide = jnp.concatenate([tile[k : k + 1] for k in range(8)], axis=1)
    return pltpu.roll(wide, 8 * LANES - at, 1)[:, :chunk]


def own_place(chunk):
    index = lax.axis_index("seq") * lax.axis_size("batch") + lax.axis_index("batch")
    return lax.rem(index * chunk, FRAME_ROWS * LANES)


def segment_ids(lengths, idk_ref, idq_ref, place, tokens):
    rows, length = idk_ref.shape[0], idk_ref.shape[1]
    upto = lax.broadcasted_iota(jnp.int32, (SEGS, LANES), 0) <= lax.broadcasted_iota(jnp.int32, (SEGS, LANES), 1)
    upto = jnp.where(upto, 1.0, 0.0).astype(BF)
    values = lengths.astype(F32)
    high = jnp.floor(values * (1.0 / 64))
    low = (values - 64.0 * high).astype(BF)
    high = high.astype(BF)
    ends = mm(high, upto) * 64.0 + mm(low, upto)
    ends = jnp.where(lax.broadcasted_iota(jnp.int32, (rows, LANES), 1) < SEGS, ends, 1e9)
    upto = upto[:, :SEGS]
    ends_down = lax.dot_general(upto, high, (((0,), (1,)), ((), ())), preferred_element_type=F32) * 64.0
    ends_down = ends_down + lax.dot_general(upto, low, (((0,), (1,)), ((), ())), preferred_element_type=F32)
    ones = jnp.ones((LANES, LANES), BF)
    span = 256
    for m in range(rows):

        def fill(i, carry, m=m):
            at = pl.multiple_of(i * span, span)
            places = (at + lax.broadcasted_iota(jnp.int32, (span, LANES), 0)).astype(F32)
            passed = jnp.where(ends[m : m + 1] <= places, 1.0, 0.0).astype(BF)
            seg = mm(passed, ones)
            idk_ref[m, pl.ds(at, span), :] = jnp.where(seg < SEGS, seg, SEGS + places)
            return carry

        lax.fori_loop(0, length // span, fill, 0)
        for h in range(H):
            first = ((h * place.parts + place.g) * tokens + lax.broadcasted_iota(jnp.int32, (1, tokens), 1)).astype(F32)
            seg = column_sum(jnp.where(ends_down[:, m : m + 1] <= first, 1.0, 0.0))
            group, k = h // GROUP, h % GROUP
            idq_ref[m, group, :, k * tokens : (k + 1) * tokens] = jnp.where(seg < SEGS, seg, SEGS + first)


def layer_kernel(
    groups_ref, lengths_ref, tok_ref, cot_ref, attn_ref, ffn_ref, params_ref, arows_ref, acols_ref, frows_ref,
    fcols_ref, sq_ref,
    out_hbm, du_hbm, agrad_hbm, fgrad_hbm, update_a_hbm, update_f_hbm, scales_ref, rows_new_ref, acols_new_ref,
    fcols_new_ref, own_new_ref,
    *scratch,
):
    place = Place()
    scratch = list(scratch)
    own_sems, recv_sems, send_sems = scratch.pop(), scratch.pop(), scratch.pop()
    wire = Wire(send_sems, recv_sems)

    def take(count):
        taken = scratch[:count]
        del scratch[:count]
        return taken

    pack_low, kv_low, wo_low, ffn_low, own_ref, small_ref, pack_ref, wkv_ref, wo_ref, w1_ref, w2_ref = take(11)
    idk_ref, idq_ref, q_ref, kv_ref, qsend_ref, kvsend_ref, qm_ref, dom_ref = take(8)
    peak_ref, acc_ref, ot_ref, lse_ref, delta_ref, o_ref, otile_ref, dotile_ref, do_ref = take(9)
    act_ref, slope_ref, dz_ref, sum_ref, frames_ref = take(5)
    dqt_ref, part_ref, near_ref, dkv_sum, dq_ref, dq_back, dkv_back = take(7)
    dwo_ref, dw1_ref, dw2_ref, dkv_w_ref, dq_w_ref, dsmall_ref = take(6)
    cols_plane, rows_plane, all_z, late_cols, late_rows, late_sums, all_sums = take(7)
    out_ref, du_ref, agrad_ref, fgrad_ref, update_a, update_f = take(6)
    written = [
        pltpu.make_async_copy(src, dst, own_sems.at[5 + i])
        for i, (src, dst) in enumerate(
            (
                (out_ref, out_hbm),
                (du_ref, du_hbm),
                (agrad_ref, agrad_hbm),
                (fgrad_ref, fgrad_hbm),
                (update_a, update_a_hbm),
                (update_f, update_f_hbm),
            )
        )
    ]
    n_z, n_b, parts = place.n_z, place.n_b, place.parts
    rows = 2
    count = tok_ref.shape[0]
    tokens = count // rows
    r, cols = attn_ref.shape[1:]
    cols_f = ffn_ref.shape[2]
    groups = H // GROUP
    width = GROUP * tokens
    keys = parts * tokens
    scale2 = SCALE * LOG2E
    low = low_half()

    plane = [(dx, db) for db in range(n_b) for dx in range(4) if dx or db]

    def plane_peer(dx, db):
        return (place.z * 4 + place.xc_ahead[dx], place.batch_ahead(db))

    along = [place.along_z(k) for k in range(1, n_z)]
    greet_all(place)

    chunk = params_ref.shape[0]
    own_at = own_place(chunk)
    own = to_frame(params_ref[...].reshape(1, chunk), own_at)
    own_ref[...] = own
    pack_low[0, :r] = attn_ref[0].astype(BF)
    tile = jnp.concatenate([own, jnp.zeros((8, LANES), F32)], axis=0)
    if cols < LANES:
        tile = jnp.concatenate([own[:, :cols], own[:, cols:]], axis=0)
    if cols > LANES:
        tile = jnp.concatenate([tile, jnp.zeros((16, cols - LANES), F32)], axis=1)
    pack_low[0, r:] = tile.astype(BF)
    pack = ShortGather(place, wire, pack_low, pack_ref, own_sems.at[0], n_z)
    kv_low[...] = attn_ref[1:3].astype(BF)
    kv_w = ShortGather(place, wire, kv_low, wkv_ref, own_sems.at[4], n_z)
    wo_low[0] = attn_ref[3].astype(BF)
    ffn_low[...] = ffn_ref[...].astype(BF)
    segment_ids(lengths_ref[...], idk_ref, idq_ref, place, tokens)
    for i in range(rows * groups):
        peak_ref[i] = jnp.full((1, width), NEG, F32)
        acc_ref[i] = jnp.zeros((HD + 16, width), F32)
    frames_ref[...] = jnp.zeros_like(frames_ref)
    dqt_ref[...] = jnp.zeros_like(dqt_ref)
    pack.to_plane()
    kv_w.to_plane()
    most = n_z - n_z // 4
    first = Gather(place, wire, ffn_low.at[pl.ds(0, 1)], w1_ref, own_sems.at[1], most)
    out_w = Gather(place, wire, wo_low, wo_ref, own_sems.at[2], most)
    second = Gather(place, wire, ffn_low.at[pl.ds(1, 1)], w2_ref, own_sems.at[3], most)
    pack.to_cores()
    pack.finish()
    frame = place.n_s * n_b // FRAMES
    for f in range(FRAMES):
        total = None
        for i in range(f * frame, (f + 1) * frame):
            s, b = i // n_b, i % n_b
            tile = pack_ref[b, 0, s // 4, s % 4, r:].astype(F32)
            if cols < LANES:
                tile = jnp.concatenate([tile[:8], tile[8:]], axis=1)
            tile = tile[:8, :LANES]
            total = tile if total is None else total + tile
        small_ref[f] = total
    lang = language_rows(groups_ref, small_ref, rows)

    def inputs():
        return jnp.concatenate(
            [tok_ref[m * tokens : (m + 1) * tokens].astype(F32) + lang[m] for m in range(rows)], axis=0
        )

    def w_qkv(b, j):
        w = wkv_ref[b, j - 1] if j else pack_ref[b, 0, :, :, :r]
        return w.reshape(D, cols)

    a = inputs().astype(BF)

    def project(j, bias):
        out = jnp.concatenate([mm(a, w_qkv(b, j)) for b in range(n_b)], axis=1)
        if bias is not None:
            out = out + small_piece(small_ref, bias, 4)
        return [t.astype(BF) for t in rows_to_heads(out[:tokens], out[tokens:])]

    for h, t in enumerate(project(0, ROW_BQ)):
        qsend_ref[h] = t
    q_ref[place.h] = qsend_ref[place.h]
    def to_heads(src, dst):
        return [
            wire.send(lambda k=k: (src.at[place.head_ahead(k)], dst.at[place.h], place.across_heads(k)))
            for k in outwards(H)
        ]

    moved_q = to_heads(qsend_ref, q_ref)
    kv_w.to_cores()
    first.to_plane()
    out_w.to_plane()
    kv_w.finish()
    for j, bias in ((0, None), (1, ROW_BV)):
        for h, t in enumerate(project(1 + j, bias)):
            kvsend_ref[h, j] = t
    kv_ref[place.s] = kvsend_ref[place.h]
    kv_sems = wire.reserve(H)
    share_sems = wire.reserve(H * (parts - 1))

    def moved_kv(i):
        k = far_first(i)
        return wire.make(
            kv_sems + i, kvsend_ref.at[place.head_ahead(k)], kv_ref.at[place.s], place.across_heads(k)
        )

    def ordered(i):
        return far_first(i) if isinstance(i, int) else jnp.where(i == 0, 0, far_first(i))

    def shared_kv(i, j):
        slot = kv_ref.at[place.head_behind(ordered(i)) * parts + place.g]
        return wire.make(share_sems + i * (parts - 1) + j - 1, slot, slot, place.across_parts(j))

    for j in range(1, parts):
        shared_kv(0, j).start()
    for k in range(1, H):
        moved_kv(k).start()
    second.to_plane()

    def masked_rows(src_ref, dst_ref):
        for g in range(groups):
            both = src_ref[g * GROUP : (g + 1) * GROUP].reshape(width, LANES)
            zero = jnp.zeros_like(both)
            dst_ref[0, g] = jnp.where(low, both, zero)
            dst_ref[1, g] = jnp.where(low, zero, both)

    received(moved_q)
    masked_rows(q_ref, qm_ref)

    def pair(h):
        kv = kv_ref[pl.ds(h * parts, parts)]
        return kv[:, 0].reshape(keys, LANES), kv[:, 1].reshape(keys, LANES)

    def key_ids(h, m):
        ids = idk_ref[m, pl.ds(pl.multiple_of(h * keys, keys), keys), :]
        return jnp.concatenate([ids] * (width // LANES), axis=1)

    def attend(k):
        h = place.head_behind(ordered(k))
        ids = [key_ids(h, m) for m in range(rows)]
        for j in range(1, parts):
            shared_kv(k, j).wait_recv()
        key, value = pair(h)
        value_t = value.T
        ones = jnp.ones((16, keys), BF)
        for g in range(groups):
            for m in range(rows):
                i = g * rows + m
                s = jnp.where(ids[m] == idq_ref[m, g], mm_nt(key, qm_ref[m, g]) * scale2, NEG)
                new = jnp.maximum(peak_ref[i], jnp.max(s, axis=0, keepdims=True))
                p = jnp.exp2(s - new).astype(BF)
                alpha = jnp.exp2(peak_ref[i] - new)
                left = jnp.concatenate([value_t[m * HD : (m + 1) * HD], ones], axis=0)
                acc_ref[i] = acc_ref[i] * alpha + mm(left, p)
                peak_ref[i] = new

    def meanwhile(k, *stages):
        for at, stage in stages:
            pl.when(k == at)(stage)

    def forward_step(k, carry):
        moved_kv(k).wait_recv()
        for j in range(1, parts):
            shared_kv(k, j).start()
        attend(k - 1)
        meanwhile(
            k,
            (2, first.to_diagonal),
            (2, out_w.to_diagonal),
            (6, second.to_diagonal),
        )
        return carry

    lax.fori_loop(1, H, forward_step, 0)
    attend(H - 1)
    for g in range(groups):
        for m in range(rows):
            i = g * rows + m
            total = acc_ref[i, HD : HD + 1]
            ot_ref[g, m * HD : (m + 1) * HD] = acc_ref[i, :HD] * (1.0 / total)
            lse_ref[i] = peak_ref[i] + jnp.log2(total)
        o_ref[g * GROUP : (g + 1) * GROUP] = ot_ref[g].T.astype(BF).reshape(GROUP, tokens, LANES)
    moved = to_heads(o_ref, otile_ref)
    otile_ref[place.h] = o_ref[place.h]
    for piece in (out_w, first, second):
        piece.to_cores()

    tiles, wide = act_ref.shape[0], act_ref.shape[2]
    per_b = cols_f // wide
    bias_1 = [small_piece(small_ref, ROW_B1 + i * wide // LANES, wide // LANES) for i in range(tiles)]
    gain1, shift1 = small_piece(small_ref, ROW_G1, 4), small_piece(small_ref, ROW_S1, 4)
    gain2, shift2 = small_piece(small_ref, ROW_G2, 4), small_piece(small_ref, ROW_S2, 4)
    bias_o, bias_2 = small_piece(small_ref, ROW_BO, 4), small_piece(small_ref, ROW_B2, 4)

    def block(ref, i):
        at = i % per_b * wide
        return ref[i // per_b, 0, :, :, :, at : at + wide].reshape(D, wide)

    live = jnp.concatenate(
        [idk_ref[m, pl.ds(pl.multiple_of(place.s * tokens, tokens), tokens), :] for m in range(rows)], axis=0
    )
    live = jnp.where(live < SEGS, 1.0, 0.0)
    u = inputs()
    out_w.finish()
    first.finish()
    received(moved)
    mixed = jnp.concatenate(heads_to_rows([otile_ref[h].astype(F32) for h in range(H)]), axis=0).astype(BF)
    attn_out = jnp.concatenate([mm(mixed, wo_ref[b, 0].reshape(D, cols)) for b in range(n_b)], axis=1)
    normed1, inverse1 = normed_of(u + (attn_out + bias_o))
    hidden = normed1 * gain1 + shift1
    hb = hidden.astype(BF)
    for i in range(tiles):
        act, slope = gelu_pair(mm(hb, block(w1_ref, i)) + bias_1[i])
        slope_ref[i] = slope
        act_ref[i] = act.astype(BF)
    second.finish()
    total = hidden + u + bias_2
    for i in range(tiles):
        total = total + mm_nt(act_ref[i], block(w2_ref, i))

    normed2, inverse2 = normed_of(total)
    out_ref[...] = (normed2 * gain2 + shift2).astype(BF)
    c = cot_ref[...].astype(F32) * jnp.concatenate([live] * (D // LANES), axis=1)
    dr = norm_back(c * gain2, normed2, inverse2)
    df = dr.astype(BF)

    def scatter(part):
        return Scatter(place, wire, part, *take(SCATTER_SCRATCH))

    g_first, g_second, g_out = scatter(dw1_ref), scatter(dw2_ref), scatter(dwo_ref)
    g_kv = scatter(dkv_w_ref)
    g_q = ShortScatter(place, wire, dq_w_ref, *take(SHORT_SCRATCH))
    g_small = ShortScatter(place, wire, dsmall_ref, *take(SHORT_SCRATCH))

    def weight_grad(left, right_ref, dst_ref):
        left = left.T
        for i in range(tiles):
            at = i % per_b * wide
            grad = mm(left, right_ref[i]).astype(BF).reshape(n_z, 2, 2, r, wide)
            dst_ref[i // per_b, 0, :, :, :, :, at : at + wide] = grad

    weight_grad(df, act_ref, dw2_ref)
    g_second.to_core()
    dh = dr
    for i in range(tiles):
        dz = (mm(df, block(w2_ref, i)) * slope_ref[i]).astype(BF)
        dz_ref[i] = dz
        dh = dh + mm_nt(dz, block(w1_ref, i))
    dpre = norm_back(dh * gain1, normed1, inverse1)
    dattn = dpre.astype(BF)
    do = mm_nt(dattn[:, :cols], wo_ref[0, 0].reshape(D, cols))
    for b in range(1, n_b):
        do = do + mm_nt(dattn[:, b * cols : (b + 1) * cols], wo_ref[b, 0].reshape(D, cols))
    for h, t in enumerate(rows_to_heads(do[:tokens], do[tokens:])):
        dotile_ref[h] = t.astype(BF)
    moved = to_heads(dotile_ref, do_ref)
    written[0].start()
    do_ref[place.h] = dotile_ref[place.h]
    sum_ref[...] = dpre + dr

    g_second.to_diagonal()
    weight_grad(hb, dz_ref, dw1_ref)
    g_first.to_core()
    mixed_t = mixed.T
    for b in range(n_b):
        dwo = mm(mixed_t, dattn[:, b * cols : (b + 1) * cols]).astype(BF)
        dwo_ref[b, 0] = dwo.reshape(n_z, 2, 2, r, cols)
    g_out.to_core()
    for k in range(H):
        for j in range(1, parts):
            shared_kv(k, j).wait_send()
        if k:
            moved_kv(k).wait_send()
    wire.drain()

    g_first.to_diagonal()
    g_out.to_diagonal()
    add_small(frames_ref, ROW_G2, column_sum(c * normed2))
    add_small(frames_ref, ROW_S2, column_sum(c))
    add_small(frames_ref, ROW_B2, column_sum(df.astype(F32)))
    for i in range(tiles):
        add_small(frames_ref, ROW_B1 + i * wide // LANES, column_sum(dz_ref[i].astype(F32)))
    add_small(frames_ref, ROW_G1, column_sum(dh * normed1))
    add_small(frames_ref, ROW_S1, column_sum(dh))
    add_small(frames_ref, ROW_BO, column_sum(dattn.astype(F32)))
    received(moved)
    masked_rows(do_ref, dom_ref)
    g_second.to_plane()
    for g in range(groups):
        product = do_ref[g * GROUP : (g + 1) * GROUP].reshape(width, LANES).astype(F32).T * ot_ref[g]
        for m in range(rows):
            delta_ref[g * rows + m] = column_sum(product[m * HD : (m + 1) * HD])

    near_sems = wire.reserve(H * (parts - 1))
    back_sems = wire.reserve(H)

    def target(k):
        far = far_first(k) if isinstance(k, int) else jnp.where(k == H, H, far_first(k))
        return place.head_ahead(far)

    def near_kv(k, j):
        h = target(k)
        return wire.make(
            near_sems + (k - 1) * (parts - 1) + j - 1,
            part_ref.at[h, place.part_ahead(j)],
            near_ref.at[j - 1, h],
            place.across_parts(j),
        )

    def back_kv(k):
        h = target(k)
        return wire.make(back_sems + k - 1, dkv_sum.at[h], dkv_back.at[place.h], (h * parts + place.g, place.b))

    def fold(k):
        h = target(k)
        total = part_ref[h, place.g].astype(F32)
        for j in range(1, parts):
            near_kv(k, j).wait_recv()
            total = total + near_ref[j - 1, h].astype(F32)
        return total.astype(BF)

    def key_step(k):
        h = target(k)
        key, value = pair(h)
        key_t = key.T
        ids = [key_ids(h, m) for m in range(rows)]
        dk = jnp.zeros((keys, LANES), F32)
        dv = jnp.zeros((keys, LANES), F32)
        for g in range(groups):
            for m in range(rows):
                i = g * rows + m
                p = jnp.exp2(mm_nt(key, qm_ref[m, g]) * scale2 - lse_ref[i])
                p = jnp.where(ids[m] == idq_ref[m, g], p, 0.0)
                ds = (p * (mm_nt(value, dom_ref[m, g]) - delta_ref[i])).astype(BF)
                dv = dv + mm(p.astype(BF), dom_ref[m, g])
                dk = dk + mm(ds, qm_ref[m, g])
                dqt_ref[g, m * HD : (m + 1) * HD] += mm(key_t[m * HD : (m + 1) * HD], ds)
        part_ref[h, :, 0] = (dk * SCALE).astype(BF).reshape(parts, tokens, LANES)
        part_ref[h, :, 1] = dv.astype(BF).reshape(parts, tokens, LANES)
        for j in range(1, parts):
            near_kv(k, j).start()

    def backward_step(k, carry):
        key_step(k)
        dkv_sum[target(k - 1)] = fold(k - 1)
        back_kv(k - 1).start()
        meanwhile(
            k,
            (6, g_first.to_plane),
            (6, g_out.to_plane),
        )
        return carry

    token_pieces = (g_second, g_first, g_out)
    key_step(1)
    lax.fori_loop(2, H + 1, backward_step, 0)
    for g in range(groups):
        dq_ref[g * GROUP : (g + 1) * GROUP] = (dqt_ref[g] * SCALE).T.astype(BF).reshape(GROUP, tokens, LANES)
    moved = to_heads(dq_ref, dq_back)
    dq_back[place.h] = dq_ref[place.h]
    dkv_back[place.h] = fold(H)
    g_second.to_owner()

    def to_rows(parts_of):
        return jnp.concatenate(heads_to_rows([t.astype(F32) for t in parts_of]), axis=0).astype(BF)

    def grad_of(left, right, b):
        return mm(left, right[:, b * cols : (b + 1) * cols]).astype(BF).reshape(n_z, 2, 2, r, cols)

    def back_through(total, right, j):
        for b in range(n_b):
            total = total + mm_nt(right[:, b * cols : (b + 1) * cols], w_qkv(b, j))
        return total

    for k in range(1, H):
        back_kv(k).wait_recv()
    a_t = inputs().astype(BF).T
    dk = to_rows([dkv_back[h, 0] for h in range(H)])
    dv = to_rows([dkv_back[h, 1] for h in range(H)])
    for b in range(n_b):
        dkv_w_ref[b, 0] = grad_of(a_t, dk, b)
        dkv_w_ref[b, 1] = grad_of(a_t, dv, b)
    g_kv.to_core()
    add_small(frames_ref, ROW_BV, column_sum(dv.astype(F32)))
    du = back_through(back_through(sum_ref[...], dk, 1), dv, 2)
    g_kv.to_diagonal()
    g_first.to_owner()
    g_out.to_owner()
    received(moved)
    dq = to_rows([dq_back[h] for h in range(H)])
    for b in range(n_b):
        dq_w_ref[b, 0] = grad_of(a_t, dq, b)
    g_q.to_core()
    du = back_through(du, dq, 0)
    add_small(frames_ref, ROW_BQ, column_sum(dq.astype(F32)))
    sums = [column_sum(du[m * tokens : (m + 1) * tokens]) for m in range(rows)]
    for e in range(GROUPS):
        total = jnp.zeros_like(sums[0])
        for m in range(rows):
            total = total + jnp.where(groups_ref[m] == e, sums[m], 0.0)
        add_small(frames_ref, ROW_E + 4 * e, total)
    for s in range(place.n_s):
        for b in range(n_b):
            dsmall_ref[b, 0, s // 4, s // 2 % 2, s % 2] = frames_ref[(s * n_b + b) // frame]
    g_small.to_core()
    g_q.to_plane()
    g_kv.to_plane()
    g_small.to_plane()
    du_ref[...] = du.astype(BF)
    written[1].start()
    g_kv.to_owner()

    weights = [attn_ref.at[j] for j in range(4)] + [ffn_ref.at[j] for j in range(2)]
    outs = [agrad_ref.at[j] for j in range(4)] + [fgrad_ref.at[j] for j in range(2)]
    updates = [update_a.at[j] for j in range(4)] + [update_f.at[j] for j in range(2)]
    old_cols = [acols_ref[j : j + 1] for j in range(4)] + [fcols_ref[j : j + 1] for j in range(2)]
    owners = [(g_q, 0), (g_kv, 0), (g_kv, 1), (g_out, 0), (g_first, 0), (g_second, 0)]
    spans = [cols] * 4 + [cols_f] * 2
    places, used = [], 0
    for span in spans:
        places.append(used)
        used += -(-span // LANES)
    pad = cols_plane.shape[1]
    late = 3
    mine = cols_plane.at[place.xc]
    mine_rows = rows_plane.at[place.b, place.xc]
    mine_late = late_cols.at[place.s]
    mine_late_rows = late_rows.at[place.b]
    mine_sums = late_sums.at[place.b, place.s]
    mine[...] = jnp.zeros((pad, LANES), F32)
    mine_late[...] = jnp.zeros((8, LANES), F32)
    lane = lax.broadcasted_iota(jnp.int32, (r, LANES), 1)
    square_sums = [None] * SLABS
    old_rows = jnp.concatenate([arows_ref[...], frows_ref[...], jnp.zeros((2, r), F32)], axis=0).T
    old_rows = [old_rows[:, j : j + 1] for j in range(SLABS)]
    row_sums_old = [sum_all(x) for x in old_rows]
    weight_squares = [sum_all(w[...] * w[...]) for w in weights]
    own = own_ref[...]
    entry = lax.broadcasted_iota(jnp.int32, (8, LANES), 0) * LANES + lax.broadcasted_iota(jnp.int32, (8, LANES), 1)
    own_mask = jnp.where((entry >= own_at) & (entry < own_at + chunk), 1.0, 0.0)
    weight_squares.append(sum_all(own * own))
    rows_tiles = []

    def gradient(j):
        owner, slab = owners[j]
        grad = owner.total(slab)
        outs[j][...] = grad
        square = grad * grad + EPS_ONE
        row_sum = jnp.sum(square, axis=1, keepdims=True)
        col_sum = column_sum(square)
        ref = mine_late if j < late else mine
        for k in range(0, spans[j], LANES):
            span = min(LANES, spans[j] - k)
            ref[pl.ds(places[j] + k // LANES, 1), pl.ds(0, span)] = col_sum[:, k : k + span]
        square_sums[j] = sum_all(row_sum)
        return jnp.where(lane == j, row_sum, 0.0)

    def renewed(j, row_total, sums, square_total, old_total):
        length = D if j < 4 else FF
        new_rows = DECAY * old_rows[j] + (1.0 - DECAY) * row_total[:, j : j + 1] * (1.0 / length)
        rows_tiles.append(jnp.where(lane == j, new_rows, 0.0))
        mean_rows = (DECAY / n_b * old_total + (1.0 - DECAY) * (1.0 / length) * square_total) * (1.0 / D)
        pieces = [
            sums[places[j] + k // LANES : places[j] + k // LANES + 1, : min(LANES, spans[j] - k)]
            for k in range(0, spans[j], LANES)
        ]
        col_sum = pieces[0] if len(pieces) == 1 else jnp.concatenate(pieces, axis=1)
        new = DECAY * old_cols[j] + (1.0 - DECAY) * (1.0 / D) * col_sum
        if j < 4:
            acols_new_ref[j : j + 1, :] = new
        else:
            fcols_new_ref[j - 4 : j - 3, :] = new
        update = outs[j][...] * lax.rsqrt((new_rows / mean_rows) * new)
        updates[j][...] = update
        return sum_all(update * update)

    def pick(tile, j):
        return tile[0:1, j : j + 1]

    def fan(i, ref, offsets):
        for db in offsets:
            b = place.batch_ahead(db)

            def one(k, carry=0, b=b):
                wire.make(i, ref, ref, (wrap(place.s + k, place.n_s), b)).start()
                return carry

            if place.n_s > 16:
                lax.fori_loop(0 if db else 1, place.n_s, one, 0)
            else:
                for k in outwards(place.n_s) + [0] * (db > 0):
                    one(k)

    near, others = [0], list(range(1, n_b))
    one_peer = place.along_z(1)

    for piece in token_pieces:
        piece.finish()
    mine_rows[pl.ds(0, r), :] = gradient(5) + gradient(4) + gradient(3)
    tail = pl.ds(r, 8)
    mine_rows[tail, :] = lanes_of(square_sums + row_sums_old + weight_squares)
    moved = []
    for dx, db in plane:
        peer = plane_peer(dx, db)
        if db == 0:
            moved.append(wire.send(lambda peer=peer: (mine, mine, peer)))
        if dx == 0:
            moved.append(wire.send(lambda peer=peer: (mine_rows, mine_rows, peer)))
        else:
            moved.append(wire.send(lambda peer=peer: (mine_rows.at[tail], mine_rows.at[tail], peer)))
    g_q.to_owner()
    g_small.to_owner()
    g_kv.finish()
    row_tile = gradient(1) + gradient(2)
    received(moved)
    mine_z = all_z.at[place.z]
    mine_z[pl.ds(0, pad), :] = cols_plane[0] + cols_plane[1] + cols_plane[2] + cols_plane[3]
    scalars = jnp.zeros((8, LANES), F32)
    row_total = jnp.zeros((r, LANES), F32)
    for b in range(n_b):
        for xc in range(4):
            scalars = scalars + rows_plane[b, xc, tail, :]
        row_total = row_total + rows_plane[b, place.xc, pl.ds(0, r), :]
    mine_z[pl.ds(pad, 8), :] = scalars
    moved = [wire.send(lambda peer=peer: (mine_z, mine_z, peer)) for peer in along]

    g_q.finish()
    mine_late_rows[...] = row_tile + gradient(0)
    written[2].start()
    written[3].start()
    sums = lanes_of(square_sums[:late])[0:1]
    mine_late[7:8, :] = sums
    late_sums[place.b] = jnp.zeros((place.n_s, 1, LANES), F32)
    mine_sums[...] = sums
    late_i, sums_i, all_i = wire.reserve(1), wire.reserve(1), wire.reserve(1)
    moved_rows = [
        wire.send(lambda k=k: (mine_late_rows, mine_late_rows, place.across_batch(k))) for k in range(1, n_b)
    ]
    fan(late_i, mine_late, near)
    fan(sums_i, mine_sums, others)

    received(moved)
    reduced = all_z[0]
    for z in range(1, n_z):
        reduced = reduced + all_z[z]
    tile = reduced[pad:]

    def scalar(j):
        return pick(tile, j)

    update_squares = [None] * SLABS
    for j in range(late, SLABS):
        update_squares[j] = renewed(j, row_total, reduced, scalar(j), scalar(SLABS + j))
    g_small.finish()
    own_grad = g_small.total(0) * own_mask
    own_sq = DECAY * to_frame(sq_ref[...].reshape(1, chunk), own_at) + (1.0 - DECAY) * (own_grad * own_grad + EPS_ONE)
    own_update = own_grad * lax.rsqrt(own_sq)
    update_squares.append(sum_all(own_update * own_update))
    for k in range(1, H + 1):
        for j in range(1, parts):
            near_kv(k, j).wait_send()
        if k < H:
            back_kv(k).wait_send()
    wire.drain()

    late_part = late_cols.at[pl.ds(0, place.n_s - 1)]
    sums_part = late_sums.at[pl.ds(0, n_b - 1)]
    wire.make(late_i, late_part, late_part, one_peer).wait_recv()
    wire.make(sums_i, sums_part, sums_part, one_peer).wait_recv()
    received(moved_rows)
    sums = late_cols[0]
    for s in range(1, place.n_s):
        sums = sums + late_cols[s]
    totals = jnp.zeros((1, LANES), F32)
    row_total = jnp.zeros((r, LANES), F32)
    for b in range(n_b):
        other = late_sums[b, 0]
        for s in range(1, place.n_s):
            other = other + late_sums[b, s]
        totals = totals + jnp.where(place.b == b, sums[7:8], other)
        row_total = row_total + late_rows[b]
    for j in range(late):
        update_squares[j] = renewed(j, row_total, sums, pick(totals, j), scalar(SLABS + j))
    written[4].start()
    written[5].start()
    rows_new_ref[...] = sum(rows_tiles[1:], rows_tiles[0])
    mine_u = all_sums.at[place.b * place.n_s + place.s]
    mine_u[...] = lanes_of(update_squares)[0:1]
    fan(all_i, mine_u, near + others)
    wire.make(late_i, late_part, late_part, one_peer).wait_send()
    wire.make(sums_i, sums_part, sums_part, one_peer).wait_send()
    all_part = all_sums.at[pl.ds(0, place.n_s * n_b - 1)]
    copy = wire.make(all_i, all_part, all_part, one_peer)
    copy.wait_send()
    copy.wait_recv()
    update_tile = jnp.zeros((1, LANES), F32)
    for i in range(place.n_s * n_b):
        update_tile = update_tile + all_sums[i]
    sizes = [D * D] * 4 + [D * FF] * 2 + [NVEC]

    def scale(j):
        weight = jnp.sqrt(scalar(2 * SLABS + j) * (1.0 / sizes[j]))
        return LEARN * weight / jnp.maximum(1.0, jnp.sqrt(update_tile[0:1, j : j + 1] * (1.0 / sizes[j])))

    scales_ref[...] = lanes_of([scale(j) for j in range(SLABS)])
    own_new_ref[0] = own_grad
    own_new_ref[1] = own - scale(SLABS) * own_update
    own_new_ref[2] = own_sq
    for copy in written:
        copy.wait()
    wire.drain()


def layer_part(groups, lengths, tok, cot, attn, ffn, params, arows, acols, frows, fcols, sq):
    n_s, n_b = lax.axis_size("seq"), lax.axis_size("batch")
    n_z, parts = n_s // 4, n_s // H
    count = tok.shape[0]
    tokens = count // 2
    rows = 2
    _, r, cols = attn.shape
    cols_f = ffn.shape[2]
    groups_q = H // GROUP
    width = GROUP * tokens
    length = tokens * n_s
    wide = min(512, cols_f)
    tiles = FF // wide
    pad = 4 * -(-cols // LANES) + 2 * (cols_f // LANES)
    pad = -(-pad // 8) * 8
    gather = (n_z - 1) + (1 + n_b) + 2 * (n_b - 1) + 1 + (n_b - 1) + 2 * (n_b - 1)
    copies = 5 * gather + 7 * (H - 1) + 2 * H + 2 * H * (parts - 1)
    copies += 6 * (1 + 2 * (n_b - 1) + n_b + n_z - 1)
    copies += 6 + 4 * n_b + (n_z - 1) + (n_b - 1) + 3

    def shape(dims, kind):
        return jax.ShapeDtypeStruct(dims, kind)

    out = (
        shape(tok.shape, BF),
        shape(tok.shape, BF),
        shape(attn.shape, F32),
        shape(ffn.shape, F32),
        shape(attn.shape, F32),
        shape(ffn.shape, F32),
        shape((8, LANES), F32),
        shape((r, LANES), F32),
        shape(acols.shape, F32),
        shape(fcols.shape, F32),
        shape((3, 8, LANES), F32),
    )
    vmem = pltpu.VMEM
    heads = (H, tokens, LANES)
    scratch = [
        vmem((1, r + 16, cols), BF),
        vmem((2, r, cols), BF),
        vmem((1, r, cols), BF),
        vmem(ffn.shape, BF),
        vmem((8, LANES), F32),
        vmem((FRAMES, 8, LANES), F32),
        vmem((n_b, 1, n_z, 4, r + 16, cols), BF),
        vmem((n_b, 2, n_z, 4, r, cols), BF),
        vmem((n_b, 1, n_z, 4, r, cols), BF),
        vmem((n_b, 1, n_z, 4, r, cols_f), BF),
        vmem((n_b, 1, n_z, 4, r, cols_f), BF),
        vmem((rows, length, LANES), F32),
        vmem((rows, groups_q, 1, width), F32),
        vmem(heads, BF),
        vmem((n_s, 2, tokens, LANES), BF),
        vmem(heads, BF),
        vmem((H, 2, tokens, LANES), BF),
        vmem((rows, groups_q, width, LANES), BF),
        vmem((rows, groups_q, width, LANES), BF),
        vmem((rows * groups_q, 1, width), F32),
        vmem((rows * groups_q, HD + 16, width), F32),
        vmem((groups_q, LANES, width), F32),
        vmem((rows * groups_q, 1, width), F32),
        vmem((rows * groups_q, 1, width), F32),
        vmem(heads, BF),
        vmem(heads, BF),
        vmem(heads, BF),
        vmem(heads, BF),
        vmem((tiles, count, wide), BF),
        vmem((tiles, count, wide), F32),
        vmem((tiles, count, wide), BF),
        vmem((count, D), F32),
        vmem((FRAMES, 8, LANES), F32),
        vmem((groups_q, LANES, width), F32),
        vmem((H, parts, 2, tokens, LANES), BF),
        vmem((parts - 1, H, 2, tokens, LANES), BF),
        vmem((H, 2, tokens, LANES), BF),
        vmem(heads, BF),
        vmem(heads, BF),
        vmem((H, 2, tokens, LANES), BF),
        vmem((n_b, 1, n_z, 2, 2, r, cols), BF),
        vmem((n_b, 1, n_z, 2, 2, r, cols_f), BF),
        vmem((n_b, 1, n_z, 2, 2, r, cols_f), BF),
        vmem((n_b, 2, n_z, 2, 2, r, cols), BF),
        vmem((n_b, 1, n_z, 2, 2, r, cols), BF),
        vmem((n_b, 1, n_z, 2, 2, 8, LANES), F32),
        vmem((4, pad, LANES), F32),
        vmem((n_b, 4, r + 8, LANES), F32),
        vmem((n_z, pad + 8, LANES), F32),
        vmem((n_s, 8, LANES), F32),
        vmem((n_b, r, LANES), F32),
        vmem((n_b, n_s, 1, LANES), F32),
        vmem((n_b * n_s, 1, LANES), F32),
        vmem(tok.shape, BF),
        vmem(tok.shape, BF),
        vmem(attn.shape, F32),
        vmem(ffn.shape, F32),
        vmem(attn.shape, F32),
        vmem(ffn.shape, F32),
    ]
    scratch += scatter_scratch(n_b, 1, n_z, r, cols_f, BF) * 2
    scratch += scatter_scratch(n_b, 1, n_z, r, cols, BF)
    scratch += scatter_scratch(n_b, 2, n_z, r, cols, BF)
    scratch += short_scratch(n_b, 1, n_z, r, cols, BF)
    scratch += short_scratch(n_b, 1, n_z, 8, LANES, F32)
    dma = pltpu.SemaphoreType.DMA
    scratch += [dma((copies,)), dma((copies,)), dma((11,))]
    return pl.pallas_call(
        layer_kernel,
        out_shape=out,
        in_specs=[SMEM_SPEC] + [VMEM_SPEC] * 11,
        out_specs=(pl.BlockSpec(memory_space=pl.ANY),) * 6 + (VMEM_SPEC,) * 5,
        scratch_shapes=scratch,
        compiler_params=pltpu.CompilerParams(
            vmem_limit_bytes=63 * 2**20, collective_id=0, has_side_effects=True
        ),
    )(groups, lengths, tok, cot, attn, ffn, params, arows, acols, frows, fcols, sq)


def result_kernel(
    out_in, du_in, agrad_in, fgrad_in, update_a, update_f, scales_ref, rows_ref, acols_in, fcols_in, own_ref,
    attn_ref, ffn_ref,
    out_ref, du_ref, agrad_ref, fgrad_ref, grad_ref, anew_ref, fnew_ref, new_ref, acopy_ref, fcopy_ref, copy_ref,
    arows_ref, acols_ref, frows_ref, fcols_ref, sq_ref,
    sems,
):
    pairs = ((out_in, out_ref), (du_in, du_ref), (agrad_in, agrad_ref), (fgrad_in, fgrad_ref))
    copies = [pltpu.make_async_copy(src, dst, sems.at[i]) for i, (src, dst) in enumerate(pairs)]
    for copy in copies:
        copy.start()
    for j in range(4):
        new = attn_ref[j] - scales_ref[0:1, j : j + 1] * update_a[j]
        anew_ref[j] = new
        acopy_ref[j] = new.astype(BF)
    for j in range(2):
        new = ffn_ref[j] - scales_ref[0:1, 4 + j : 5 + j] * update_f[j]
        fnew_ref[j] = new
        fcopy_ref[j] = new.astype(BF)
    rows = rows_ref[...].T
    arows_ref[...] = rows[0:4]
    frows_ref[...] = rows[4:6]
    acols_ref[...] = acols_in[...]
    fcols_ref[...] = fcols_in[...]
    chunk = grad_ref.shape[0]
    at = own_place(chunk)
    grad_ref[...] = from_frame(own_ref[0], at, chunk).reshape(chunk)
    new = from_frame(own_ref[1], at, chunk)
    new_ref[...] = new.reshape(chunk)
    copy_ref[...] = new.astype(BF).reshape(chunk)
    sq_ref[...] = from_frame(own_ref[2], at, chunk).reshape(chunk)
    for copy in copies:
        copy.wait()


def result_part(made, attn, ffn, chunk):
    out, _, agrad, fgrad, _, _, _, rows, acols, fcols, _ = made
    r = rows.shape[0]

    def shape(dims, kind):
        return jax.ShapeDtypeStruct(dims, kind)

    shapes = (
        shape(out.shape, BF),
        shape(out.shape, BF),
        shape(attn.shape, F32),
        shape(ffn.shape, F32),
        shape((chunk,), F32),
        shape(attn.shape, F32),
        shape(ffn.shape, F32),
        shape((chunk,), F32),
        shape(attn.shape, BF),
        shape(ffn.shape, BF),
        shape((chunk,), BF),
        shape((4, r), F32),
        shape(acols.shape, F32),
        shape((2, r), F32),
        shape(fcols.shape, F32),
        shape((chunk,), F32),
    )
    return pl.pallas_call(
        result_kernel,
        out_shape=shapes,
        in_specs=[VMEM_SPEC] * 13,
        out_specs=(pl.BlockSpec(memory_space=pl.ANY),) * 4 + (VMEM_SPEC,) * 12,
        scratch_shapes=[pltpu.SemaphoreType.DMA((4,))],
        compiler_params=pltpu.CompilerParams(vmem_limit_bytes=60 * 2**20),
    )(*made, attn, ffn)


def shards(
    tokens, lengths, groups, cotangent, attn_weights, ffn_weights, small_params,
    attn_rows, attn_cols, ffn_rows, ffn_cols, small_sq,
):
    micro, rb, toks, _ = tokens.shape
    rows = micro * rb
    chunk = small_params.shape[0]
    made = layer_part(
        groups.reshape(rows),
        lengths.reshape(rows, SEGS),
        tokens.reshape(rows * toks, D),
        cotangent.reshape(rows * toks, D),
        attn_weights,
        ffn_weights,
        small_params,
        attn_rows,
        attn_cols,
        ffn_rows,
        ffn_cols,
        small_sq,
    )
    results = list(result_part(made, attn_weights, ffn_weights, chunk))
    for i in (0, 1):
        results[i] = results[i].reshape(tokens.shape)
    return tuple(results)


def solution(mesh):
    acts = P(None, "batch", "seq", None)
    weights = P(None, "seq", "batch")
    small = P(("seq", "batch"))
    rows, cols = P(None, "seq"), P(None, "batch")
    return jax.shard_map(
        shards,
        mesh=mesh,
        in_specs=(acts, P(None, "batch", None), P(None, "batch"), acts, weights, weights, small)
        + (rows, cols, rows, cols, small),
        out_specs=(acts, acts, weights, weights, small, weights, weights, small, weights, weights, small)
        + (rows, cols, rows, cols, small),
        check_vma=False,
    )
```

time: 1290 us -> 141 us (0.11)
  waiting for transfers between devices: 478 us -> 0 us
  other arithmetic: 223 us -> 0 us
  blocking collectives: 203 us -> 0 us
  local copies, waits for them, and re-layouts: 198 us -> 0 us
  matrix products: 149 us -> 0 us
  Pallas kernels: 0 us -> 140 us
  between operations: 20 us -> 0.82 us
    ppermute x124 -> x0, waiting for transfers between devices: 150 us -> none  [from_behind(): return lax.ppermute(block, axis, route)]
    dot_general x218 -> x0, matrix products: 149 us -> none  [the longest x48 39.5 us: scorer(): jnp.einsum('rqhd,rkhd->rhqk', query_four, key_four, preferred_element_typ...]
    pallas_call x0 -> x2, Pallas kernels: none -> 140 us  [the longest x1 137 us: layer_part(): pl.pallas_call(layer_kernel, out_shape=out, in_specs=[SMEM_SPEC] + [VMEM_...]
    all_gather x6 -> x0, waiting for transfers between devices: 128 us -> none  [the longest x2 61.3 us: micro_pass(): lax.all_gather(value_rows, 'seq', axis=1, tiled=True)]
    convert_element_type x130 -> x0, other arithmetic: 109 us -> none  [the longest x64 49.3 us: shortened(): a.astype(jnp.bfloat16)]
    reduce_scatter x4 -> x0, waiting for transfers between devices: 100 us -> none  [the longest x2 100 us: scatter_grads(): lax.psum_scatter(ffn_part.astype(jnp.bfloat16), 'seq', scatter_dimension=...]
    psum x3 -> x0, blocking collectives: 99.8 us -> none  [the longest x1 57.6 us: shards(): lax.psum((jnp.sum(attn_square, axis=1), jnp.sum(ffn_square, axis=1), jnp....]
    unnamed x16 -> x0, waiting for transfers between devices: 99.6 us -> none
  transfers between devices with their start and end apart: 137 -> 0, of which waited for: 69 -> 0; matrix products, arithmetic and copies ran while one was open for 36% -> 0% of each run, Pallas kernels for 0% -> 0%
where the time goes in v1:
time: 141 us
  Pallas kernels  140 us (99%)
    pallas_call x1, Pallas kernels, layer_part(): pl.pallas_call(layer_kernel, out_shape=out, in_specs=[SMEM_SPEC] + [VMEM_...  137 us
    pallas_call x1, Pallas kernels, result_part(): pl.pallas_call(result_kernel, out_shape=shapes, in_specs=[VMEM_SPEC] * 13...  3.24 us

profile of v1, /device:TPU:0, one launch (start us, length us, event | category | flops | bytes accessed | tf_op | source)
XLA Modules:
  0.0 140.7 jit_solution(15932272015106523417)
XLA Ops:
  0.7 136.6 %shard_map.243 = (bf16[256,512]{1,0:T(8,128)(2,1)}, bf16[256,512]{1,0:T(8,128)(2,1)}, f32[4,32,256]{2,1,0:T(8,128)}, f32[2,32,1024]{2,1,0:T(8,128)}, f32[4,32,25...) custom-call(s32[2]{0:T(128)} %bitcast.13, ...), custom_call_target="tpu_custom_call" | custom-call | tf_op jit(solution)/shard_map/pallas_call | solution.py:1342
  137.3 3.2 %shard_map.244 = (bf16[256,512]{1,0:T(8,128)(2,1)}, bf16[256,512]{1,0:T(8,128)(2,1)}, f32[4,32,256]{2,1,0:T(8,128)}, f32[2,32,1024]{2,1,0:T(8,128)}, f32[320]{0:...) custom-call(bf16[256,512]{1,0:T(8,128)(2,1)} %get-tuple-element.43.o, ...), custom_call_target="tpu_custom_call" | custom-call | tf_op jit(solution)/shard_map/pallas_call | solution.py:1414

commit v2 on v1

--- a/solution.py
+++ b/solution.py
@@ -111,6 +111,8 @@
         self.xc_ahead = [wrap(self.xc + k, 4) for k in range(4)]
         self.h_ahead = [wrap(self.h + k, H) for k in range(H)]
         self.g_ahead = [wrap(self.g + k, self.parts) for k in range(self.parts)]
+        self.z_pair = self.z + 1 - self.z % 2 * 2
+        self.z_pair_ahead = [wrap(self.z_pair + k, self.n_z) for k in range(self.n_z)]
         self.at_z = [z * 4 + self.xc for z in self.z_ahead]
         self.at_x, self.at_core = self.z * 4 + self.other_x, self.z * 4 + self.other_c
         self.at_head = [h * self.parts + self.g for h in self.h_ahead]
@@ -118,6 +120,9 @@
 
     def along_z(self, k):
         return (self.at_z[k], self.b)
+
+    def across_z(self):
+        return (self.z_pair * 4 + self.xc, self.b)
 
     def across_x(self):
         return (self.at_x, self.b)
@@ -235,7 +240,11 @@
     def __init__(self, place, wire, src, dst, own_sem, cut):
         self.place, self.wire, self.src, self.dst, self.cut, self.own_sem = place, wire, src, dst, cut, own_sem
         self.own().start()
-        self.along = [wire.send(lambda k=k: (src, self.slot(place.z), place.along_z(k))) for k in range(1, place.n_z)]
+        self.begin()
+
+    def begin(self):
+        p = self.place
+        self.along = [self.wire.send(lambda k=k: (self.src, self.slot(p.z), p.along_z(k))) for k in range(1, p.n_z)]
 
     def slot(self, z):
         return self.dst.at[self.place.b, :, z, self.place.xc]
@@ -284,6 +293,21 @@
 
     def finish(self):
         received(self.cores)
+
+
+class PairGather(Gather):
+
+    def begin(self):
+        p, self.far = self.place, range(2, self.place.n_z, 2)
+        self.along = [self.wire.send(lambda: (self.src, self.slot(p.z), p.across_z()))]
+        self.arriving = [self.wire.send(lambda k=k: (self.src, self.slot(p.z), p.along_z(k))) for k in self.far]
+
+    def to_pair(self):
+        p = self.place
+        for copy, k in zip(self.arriving, self.far):
+            copy.wait_recv()
+            z = p.z_ahead[p.n_z - k]
+            self.along.append(self.wire.send(lambda z=z: (self.slot(z), self.slot(z), p.across_z())))
 
 
 class ShortGather(Gather):
@@ -466,6 +490,49 @@
 
     def finish(self):
         received(self.moved)
+
+
+class PairScatter(Scatter):
+
+    def to_owner(self):
+        p = self.place
+        received(self.moved)
+        self.each(lambda j, z: self.add(self.acc.at[p.b, j, z, self.x], *self.others(j, z)))
+        self.moved = [
+            self.wire.send(
+                lambda i=i: (
+                    self.acc.at[p.b, :, p.z_pair_ahead[2 * i], self.x],
+                    self.column.at[i],
+                    p.across_z(),
+                )
+            )
+            for i in range(p.n_z // 2)
+        ]
+
+    def to_far(self):
+        p = self.place
+        half = p.n_z // 2
+        received(self.moved)
+        for i in range(half):
+            for j in range(self.slabs):
+                self.add(self.acc.at[p.b, j, p.z_ahead[2 * i], self.x], self.column.at[i, j])
+        self.moved = [
+            self.wire.send(
+                lambda i=i: (
+                    self.acc.at[p.b, :, p.z_ahead[2 * i], self.x],
+                    self.column.at[half + i - 1],
+                    p.along_z(2 * i),
+                )
+            )
+            for i in range(1, half)
+        ]
+
+    def total(self, j):
+        p = self.place
+        out = self.acc[p.b, j, p.z, self.x].astype(F32)
+        for k in range(p.n_z // 2, p.n_z - 1):
+            out = out + self.column[k, j].astype(F32)
+        return out
 
 
 class ShortScatter(Scatter):
@@ -666,7 +733,7 @@
     most = n_z - n_z // 4
     first = Gather(place, wire, ffn_low.at[pl.ds(0, 1)], w1_ref, own_sems.at[1], most)
     out_w = Gather(place, wire, wo_low, wo_ref, own_sems.at[2], most)
-    second = Gather(place, wire, ffn_low.at[pl.ds(1, 1)], w2_ref, own_sems.at[3], most)
+    second = PairGather(place, wire, ffn_low.at[pl.ds(1, 1)], w2_ref, own_sems.at[3], most)
     pack.to_cores()
     pack.finish()
     frame = place.n_s * n_b // FRAMES
@@ -709,6 +776,7 @@
         ]
 
     moved_q = to_heads(qsend_ref, q_ref)
+    second.to_pair()
     kv_w.to_cores()
     first.to_plane()
     out_w.to_plane()
@@ -847,10 +915,10 @@
     df = dr.astype(BF)
 
     def scatter(part):
-        return Scatter(place, wire, part, *take(SCATTER_SCRATCH))
+        return PairScatter(place, wire, part, *take(SCATTER_SCRATCH))
 
     g_first, g_second, g_out = scatter(dw1_ref), scatter(dw2_ref), scatter(dwo_ref)
-    g_kv = scatter(dkv_w_ref)
+    g_kv = Scatter(place, wire, dkv_w_ref, *take(SCATTER_SCRATCH))
     g_q = ShortScatter(place, wire, dq_w_ref, *take(SHORT_SCRATCH))
     g_small = ShortScatter(place, wire, dsmall_ref, *take(SHORT_SCRATCH))
 
@@ -1006,6 +1074,7 @@
     add_small(frames_ref, ROW_BV, column_sum(dv.astype(F32)))
     du = back_through(back_through(sum_ref[...], dk, 1), dv, 2)
     g_kv.to_diagonal()
+    g_second.to_far()
     g_first.to_owner()
     g_out.to_owner()
     received(moved)
@@ -1028,6 +1097,8 @@
     g_q.to_plane()
     g_kv.to_plane()
     g_small.to_plane()
+    g_first.to_far()
+    g_out.to_far()
     du_ref[...] = du.astype(BF)
     written[1].start()
     g_kv.to_owner()
@@ -1116,9 +1187,13 @@
     near, others = [0], list(range(1, n_b))
     one_peer = place.along_z(1)
 
-    for piece in token_pieces:
-        piece.finish()
-    mine_rows[pl.ds(0, r), :] = gradient(5) + gradient(4) + gradient(3)
+    g_second.finish()
+    row_tile = gradient(5)
+    g_q.to_owner()
+    g_small.to_owner()
+    g_first.finish()
+    g_out.finish()
+    mine_rows[pl.ds(0, r), :] = row_tile + gradient(4) + gradient(3)
     tail = pl.ds(r, 8)
     mine_rows[tail, :] = lanes_of(square_sums + row_sums_old + weight_squares)
     moved = []
@@ -1130,8 +1205,6 @@
             moved.append(wire.send(lambda peer=peer: (mine_rows, mine_rows, peer)))
         else:
             moved.append(wire.send(lambda peer=peer: (mine_rows.at[tail], mine_rows.at[tail], peer)))
-    g_q.to_owner()
-    g_small.to_owner()
     g_kv.finish()
     row_tile = gradient(1) + gradient(2)
     received(moved)
@@ -1356,12 +1429,9 @@
     attn_ref, ffn_ref,
     out_ref, du_ref, agrad_ref, fgrad_ref, grad_ref, anew_ref, fnew_ref, new_ref, acopy_ref, fcopy_ref, copy_ref,
     arows_ref, acols_ref, frows_ref, fcols_ref, sq_ref,
-    sems,
 ):
-    pairs = ((out_in, out_ref), (du_in, du_ref), (agrad_in, agrad_ref), (fgrad_in, fgrad_ref))
-    copies = [pltpu.make_async_copy(src, dst, sems.at[i]) for i, (src, dst) in enumerate(pairs)]
-    for copy in copies:
-        copy.start()
+    for src, dst in ((out_in, out_ref), (du_in, du_ref), (agrad_in, agrad_ref), (fgrad_in, fgrad_ref)):
+        dst[...] = src[...]
     for j in range(4):
         new = attn_ref[j] - scales_ref[0:1, j : j + 1] * update_a[j]
         anew_ref[j] = new
@@ -1382,8 +1452,6 @@
     new_ref[...] = new.reshape(chunk)
     copy_ref[...] = new.astype(BF).reshape(chunk)
     sq_ref[...] = from_frame(own_ref[2], at, chunk).reshape(chunk)
-    for copy in copies:
-        copy.wait()
 
 
 def result_part(made, attn, ffn, chunk):
@@ -1415,8 +1483,7 @@
         result_kernel,
         out_shape=shapes,
         in_specs=[VMEM_SPEC] * 13,
-        out_specs=(pl.BlockSpec(memory_space=pl.ANY),) * 4 + (VMEM_SPEC,) * 12,
-        scratch_shapes=[pltpu.SemaphoreType.DMA((4,))],
+        out_specs=(VMEM_SPEC,) * 16,
         compiler_params=pltpu.CompilerParams(vmem_limit_bytes=60 * 2**20),
     )(*made, attn, ffn)
 

time: 141 us -> 137 us (0.972)
  Pallas kernels: 140 us -> 136 us
    pallas_call x1, Pallas kernels: 137 us -> 134 us  [layer_part(): pl.pallas_call(layer_kernel, out_shape=out, in_specs=[SMEM_SPEC] + [VMEM_...]
where the time goes in v2:
time: 137 us
  Pallas kernels  136 us (99%)
    pallas_call x1, Pallas kernels, layer_part(): pl.pallas_call(layer_kernel, out_shape=out, in_specs=[SMEM_SPEC] + [VMEM_...  134 us

profile of v2, /device:TPU:0, one launch (start us, length us, event | category | flops | bytes accessed | tf_op | source)
XLA Modules:
  0.0 137.1 jit_solution(6960448519600868533)
XLA Ops:
  0.7 133.6 %shard_map.243 = (bf16[256,512]{1,0:T(8,128)(2,1)}, bf16[256,512]{1,0:T(8,128)(2,1)}, f32[4,32,256]{2,1,0:T(8,128)}, f32[2,32,1024]{2,1,0:T(8,128)}, f32[4,32,25...) custom-call(s32[2]{0:T(128)} %bitcast.13, ...), custom_call_target="tpu_custom_call" | custom-call | tf_op jit(solution)/shard_map/pallas_call | solution.py:1415
  134.3 2.7 %shard_map.244 = (bf16[256,512]{1,0:T(8,128)(2,1)}, bf16[256,512]{1,0:T(8,128)(2,1)}, f32[4,32,256]{2,1,0:T(8,128)}, f32[2,32,1024]{2,1,0:T(8,128)}, f32[320]{0:...) custom-call(bf16[256,512]{1,0:T(8,128)(2,1)} %get-tuple-element.43.o, ...), custom_call_target="tpu_custom_call" | custom-call | tf_op jit(solution)/shard_map/pallas_call | solution.py:1482

commit v3 on v2

--- a/solution.py
+++ b/solution.py
@@ -172,7 +172,7 @@
 
     for k, b in enumerate(place.b_ahead):
         lax.fori_loop(0 if k else 1, place.n_s, functools.partial(hello, b), 0)
-    pl.semaphore_wait(barrier, place.n_s * place.n_b - 1)
+    return lambda: pl.semaphore_wait(barrier, place.n_s * place.n_b - 1)
 
 
 def far_first(i):
@@ -704,7 +704,7 @@
         return (place.z * 4 + place.xc_ahead[dx], place.batch_ahead(db))
 
     along = [place.along_z(k) for k in range(1, n_z)]
-    greet_all(place)
+    all_here = greet_all(place)
 
     chunk = params_ref.shape[0]
     own_at = own_place(chunk)
@@ -717,8 +717,9 @@
     if cols > LANES:
         tile = jnp.concatenate([tile, jnp.zeros((16, cols - LANES), F32)], axis=1)
     pack_low[0, r:] = tile.astype(BF)
+    kv_low[...] = attn_ref[1:3].astype(BF)
+    all_here()
     pack = ShortGather(place, wire, pack_low, pack_ref, own_sems.at[0], n_z)
-    kv_low[...] = attn_ref[1:3].astype(BF)
     kv_w = ShortGather(place, wire, kv_low, wkv_ref, own_sems.at[4], n_z)
     wo_low[0] = attn_ref[3].astype(BF)
     ffn_low[...] = ffn_ref[...].astype(BF)
@@ -731,8 +732,8 @@
     pack.to_plane()
     kv_w.to_plane()
     most = n_z - n_z // 4
-    first = Gather(place, wire, ffn_low.at[pl.ds(0, 1)], w1_ref, own_sems.at[1], most)
-    out_w = Gather(place, wire, wo_low, wo_ref, own_sems.at[2], most)
+    first = PairGather(place, wire, ffn_low.at[pl.ds(0, 1)], w1_ref, own_sems.at[1], most)
+    out_w = PairGather(place, wire, wo_low, wo_ref, own_sems.at[2], most)
     second = PairGather(place, wire, ffn_low.at[pl.ds(1, 1)], w2_ref, own_sems.at[3], most)
     pack.to_cores()
     pack.finish()
@@ -748,6 +749,8 @@
             total = tile if total is None else total + tile
         small_ref[f] = total
     lang = language_rows(groups_ref, small_ref, rows)
+    first.to_pair()
+    out_w.to_pair()
 
     def inputs():
         return jnp.concatenate(
@@ -885,6 +888,9 @@
     def block(ref, i):
         at = i % per_b * wide
         return ref[i // per_b, 0, :, :, :, at : at + wide].reshape(D, wide)
+
+    def joined(ref, b):
+        return jnp.concatenate([ref[b * per_b + i] for i in range(per_b)], axis=1)
 
     live = jnp.concatenate(
         [idk_ref[m, pl.ds(pl.multiple_of(place.s * tokens, tokens), tokens), :] for m in range(rows)], axis=0
@@ -905,8 +911,8 @@
         act_ref[i] = act.astype(BF)
     second.finish()
     total = hidden + u + bias_2
-    for i in range(tiles):
-        total = total + mm_nt(act_ref[i], block(w2_ref, i))
+    for b in range(n_b):
+        total = total + mm_nt(joined(act_ref, b), w2_ref[b, 0].reshape(D, cols_f))
 
     normed2, inverse2 = normed_of(total)
     out_ref[...] = (normed2 * gain2 + shift2).astype(BF)
@@ -935,7 +941,8 @@
     for i in range(tiles):
         dz = (mm(df, block(w2_ref, i)) * slope_ref[i]).astype(BF)
         dz_ref[i] = dz
-        dh = dh + mm_nt(dz, block(w1_ref, i))
+    for b in range(n_b):
+        dh = dh + mm_nt(joined(dz_ref, b), w1_ref[b, 0].reshape(D, cols_f))
     dpre = norm_back(dh * gain1, normed1, inverse1)
     dattn = dpre.astype(BF)
     do = mm_nt(dattn[:, :cols], wo_ref[0, 0].reshape(D, cols))

time: 137 us -> 136 us (level)
    pallas_call x1, Pallas kernels: 134 us -> 132 us  [layer_part(): pl.pallas_call(layer_kernel, out_shape=out, in_specs=[SMEM_SPEC] + [VMEM_...]
where the time goes in v3:
time: 136 us; the launch traced here: 135 us
  Pallas kernels  135 us (99%)
    pallas_call x1, Pallas kernels, layer_part(): pl.pallas_call(layer_kernel, out_shape=out, in_specs=[SMEM_SPEC] + [VMEM_...  132 us

profile of v3, /device:TPU:0, one launch (start us, length us, event | category | flops | bytes accessed | tf_op | source)
XLA Modules:
  0.0 135.5 jit_solution(796453323336351738)
XLA Ops:
  0.7 132.0 %shard_map.243 = (bf16[256,512]{1,0:T(8,128)(2,1)}, bf16[256,512]{1,0:T(8,128)(2,1)}, f32[4,32,256]{2,1,0:T(8,128)}, f32[2,32,1024]{2,1,0:T(8,128)}, f32[4,32,25...) custom-call(s32[2]{0:T(128)} %bitcast.13, ...), custom_call_target="tpu_custom_call" | custom-call | tf_op jit(solution)/shard_map/pallas_call | solution.py:1422
  132.7 2.7 %shard_map.244 = (bf16[256,512]{1,0:T(8,128)(2,1)}, bf16[256,512]{1,0:T(8,128)(2,1)}, f32[4,32,256]{2,1,0:T(8,128)}, f32[2,32,1024]{2,1,0:T(8,128)}, f32[320]{0:...) custom-call(bf16[256,512]{1,0:T(8,128)(2,1)} %get-tuple-element.43.o, ...), custom_call_target="tpu_custom_call" | custom-call | tf_op jit(solution)/shard_map/pallas_call | solution.py:1489

commit v4 on v3

--- a/solution.py
+++ b/solution.py
@@ -860,7 +860,7 @@
             k,
             (2, first.to_diagonal),
             (2, out_w.to_diagonal),
-            (6, second.to_diagonal),
+            (H - 1, second.to_diagonal),
         )
         return carry
 
@@ -1214,18 +1214,6 @@
             moved.append(wire.send(lambda peer=peer: (mine_rows.at[tail], mine_rows.at[tail], peer)))
     g_kv.finish()
     row_tile = gradient(1) + gradient(2)
-    received(moved)
-    mine_z = all_z.at[place.z]
-    mine_z[pl.ds(0, pad), :] = cols_plane[0] + cols_plane[1] + cols_plane[2] + cols_plane[3]
-    scalars = jnp.zeros((8, LANES), F32)
-    row_total = jnp.zeros((r, LANES), F32)
-    for b in range(n_b):
-        for xc in range(4):
-            scalars = scalars + rows_plane[b, xc, tail, :]
-        row_total = row_total + rows_plane[b, place.xc, pl.ds(0, r), :]
-    mine_z[pl.ds(pad, 8), :] = scalars
-    moved = [wire.send(lambda peer=peer: (mine_z, mine_z, peer)) for peer in along]
-
     g_q.finish()
     mine_late_rows[...] = row_tile + gradient(0)
     written[2].start()
@@ -1240,6 +1228,18 @@
     ]
     fan(late_i, mine_late, near)
     fan(sums_i, mine_sums, others)
+
+    received(moved)
+    mine_z = all_z.at[place.z]
+    mine_z[pl.ds(0, pad), :] = cols_plane[0] + cols_plane[1] + cols_plane[2] + cols_plane[3]
+    scalars = jnp.zeros((8, LANES), F32)
+    row_total = jnp.zeros((r, LANES), F32)
+    for b in range(n_b):
+        for xc in range(4):
+            scalars = scalars + rows_plane[b, xc, tail, :]
+        row_total = row_total + rows_plane[b, place.xc, pl.ds(0, r), :]
+    mine_z[pl.ds(pad, 8), :] = scalars
+    moved = [wire.send(lambda peer=peer: (mine_z, mine_z, peer)) for peer in along]
 
     received(moved)
     reduced = all_z[0]

time: 136 us -> 133 us (0.978)
  Pallas kernels: 135 us -> 132 us
    pallas_call x1, Pallas kernels: 132 us -> 130 us  [layer_part(): pl.pallas_call(layer_kernel, out_shape=out, in_specs=[SMEM_SPEC] + [VMEM_...]
where the time goes in v4:
time: 133 us
  Pallas kernels  132 us (99%)
    pallas_call x1, Pallas kernels, layer_part(): pl.pallas_call(layer_kernel, out_shape=out, in_specs=[SMEM_SPEC] + [VMEM_...  130 us
    pallas_call x1, Pallas kernels, result_part(): pl.pallas_call(result_kernel, out_shape=shapes, in_specs=[VMEM_SPEC] * 13...  2.66 us

profile of v4, /device:TPU:0, one launch (start us, length us, event | category | flops | bytes accessed | tf_op | source)
XLA Modules:
  0.0 133.2 jit_solution(9017125219945309622)
XLA Ops:
  0.7 129.7 %shard_map.243 = (bf16[256,512]{1,0:T(8,128)(2,1)}, bf16[256,512]{1,0:T(8,128)(2,1)}, f32[4,32,256]{2,1,0:T(8,128)}, f32[2,32,1024]{2,1,0:T(8,128)}, f32[4,32,25...) custom-call(s32[2]{0:T(128)} %bitcast.13, ...), custom_call_target="tpu_custom_call" | custom-call | tf_op jit(solution)/shard_map/pallas_call | solution.py:1422
  130.4 2.7 %shard_map.244 = (bf16[256,512]{1,0:T(8,128)(2,1)}, bf16[256,512]{1,0:T(8,128)(2,1)}, f32[4,32,256]{2,1,0:T(8,128)}, f32[2,32,1024]{2,1,0:T(8,128)}, f32[320]{0:...) custom-call(bf16[256,512]{1,0:T(8,128)(2,1)} %get-tuple-element.43.o, ...), custom_call_target="tpu_custom_call" | custom-call | tf_op jit(solution)/shard_map/pallas_call | solution.py:1489

commit v5 on v4

--- a/solution.py
+++ b/solution.py
@@ -924,7 +924,7 @@
         return PairScatter(place, wire, part, *take(SCATTER_SCRATCH))
 
     g_first, g_second, g_out = scatter(dw1_ref), scatter(dw2_ref), scatter(dwo_ref)
-    g_kv = Scatter(place, wire, dkv_w_ref, *take(SCATTER_SCRATCH))
+    g_kv = ShortScatter(place, wire, dkv_w_ref, *take(SHORT_SCRATCH))
     g_q = ShortScatter(place, wire, dq_w_ref, *take(SHORT_SCRATCH))
     g_small = ShortScatter(place, wire, dsmall_ref, *take(SHORT_SCRATCH))
 
@@ -1080,7 +1080,7 @@
     g_kv.to_core()
     add_small(frames_ref, ROW_BV, column_sum(dv.astype(F32)))
     du = back_through(back_through(sum_ref[...], dk, 1), dv, 2)
-    g_kv.to_diagonal()
+    g_kv.to_plane()
     g_second.to_far()
     g_first.to_owner()
     g_out.to_owner()
@@ -1102,7 +1102,6 @@
             dsmall_ref[b, 0, s // 4, s // 2 % 2, s % 2] = frames_ref[(s * n_b + b) // frame]
     g_small.to_core()
     g_q.to_plane()
-    g_kv.to_plane()
     g_small.to_plane()
     g_first.to_far()
     g_out.to_far()
@@ -1414,7 +1413,7 @@
     ]
     scratch += scatter_scratch(n_b, 1, n_z, r, cols_f, BF) * 2
     scratch += scatter_scratch(n_b, 1, n_z, r, cols, BF)
-    scratch += scatter_scratch(n_b, 2, n_z, r, cols, BF)
+    scratch += short_scratch(n_b, 2, n_z, r, cols, BF)
     scratch += short_scratch(n_b, 1, n_z, r, cols, BF)
     scratch += short_scratch(n_b, 1, n_z, 8, LANES, F32)
     dma = pltpu.SemaphoreType.DMA

time: 133 us -> 133 us (level)
  no operation moved by 1% of the time
where the time goes in v5:
time: 133 us
  Pallas kernels  132 us (99%)
    pallas_call x1, Pallas kernels, layer_part(): pl.pallas_call(layer_kernel, out_shape=out, in_specs=[SMEM_SPEC] + [VMEM_...  130 us
    pallas_call x1, Pallas kernels, result_part(): pl.pallas_call(result_kernel, out_shape=shapes, in_specs=[VMEM_SPEC] * 13...  2.66 us

profile of v5, /device:TPU:0, one launch (start us, length us, event | category | flops | bytes accessed | tf_op | source)
XLA Modules:
  0.0 133.3 jit_solution(16465619885892592930)
XLA Ops:
  0.7 129.8 %shard_map.243 = (bf16[256,512]{1,0:T(8,128)(2,1)}, bf16[256,512]{1,0:T(8,128)(2,1)}, f32[4,32,256]{2,1,0:T(8,128)}, f32[2,32,1024]{2,1,0:T(8,128)}, f32[4,32,25...) custom-call(s32[2]{0:T(128)} %bitcast.13, ...), custom_call_target="tpu_custom_call" | custom-call | tf_op jit(solution)/shard_map/pallas_call | solution.py:1421
  130.5 2.7 %shard_map.244 = (bf16[256,512]{1,0:T(8,128)(2,1)}, bf16[256,512]{1,0:T(8,128)(2,1)}, f32[4,32,256]{2,1,0:T(8,128)}, f32[2,32,1024]{2,1,0:T(8,128)}, f32[320]{0:...) custom-call(bf16[256,512]{1,0:T(8,128)(2,1)} %get-tuple-element.43.o, ...), custom_call_target="tpu_custom_call" | custom-call | tf_op jit(solution)/shard_map/pallas_call | solution.py:1488
